TPU v7x, 512 devices: a whole 4x8x8 slice. The times are simulated.
512 devices in a mesh: req: 32 (over y, x), seq: 16 (over z, core).
Axes of the slice: x: 4, y: 8, z: 8, core: 2. Of those that a mesh axis runs over, the one named last changes fastest.
Arguments:
- queries: bfloat16 [65536, 4096], P(('req', 'seq')), parts along dimension 0, may hold values from -6 to 6
- span_keys: bfloat16 [65536, 512], P(('req', 'seq')), parts along dimension 0, may hold values from -6 to 6
- span_values: bfloat16 [65536, 512], P(('req', 'seq')), parts along dimension 0, may hold values from -6 to 6
- cache_keys: bfloat16 [65536, 512], P(('req', 'seq')), parts along dimension 0, may hold values from -6 to 6
- cache_values: bfloat16 [65536, 512], P(('req', 'seq')), parts along dimension 0, may hold values from -6 to 6
- block_lists: int32 [512, 32, 4], P(('req', 'seq')), parts along dimension 0, may hold values from 0 to 31, as said below
Outputs:
- attended: bfloat16 [65536, 4096], P(('req', 'seq')), parts along dimension 0
There are 32 independent parts, one for each index of `req`. A program takes and returns all parts, laid end to end along the dimension named above; each array names one. Nothing has to cross between parts.
Inputs may be any that keep to these rules, and one draw needn't show every extreme that they name: block_lists[i, h] holds 4 different key block indices, none above 16 + i; it always holds block 0 and the blocks 16 + i - 1 to 16 + i.
All inputs are finite; a program needn't handle non-finite values.
Results may differ from a plain program's by a relative error of at most 0.0049.
Values may be sent and summed in bfloat16 or wider, within the bound.
No kernel may reach another device: no remote copies, remote signals or barrier semaphores. Data moves between devices by JAX's collectives and lax.ppermute only.
A program may use at most 64 MiB of HBM per device.

v0:
```python
import math

import jax
import jax.numpy as jnp
from jax import lax
from jax.sharding import PartitionSpec as P

QUERY_HEADS_HALF = 32
KVH = 4
DH = 128
BLK = 128


def attend(
    query_blocks, block_list, offsets, key_blocks, value_blocks, kv_of_head, group_size, cache_len
):
    heads_here = query_blocks.shape[2]
    per_group = min(heads_here, group_size)
    tokens_block = query_blocks.shape[1]
    score_scale = 1.0 / math.sqrt(query_blocks.shape[3])

    def one_block(member):
        query_block, head_lists, offset = member
        pieces = []
        for first in range(0, heads_here, per_group):
            own_lists = head_lists[first : first + per_group]
            own_heads = kv_of_head[first : first + per_group]
            picked_keys = key_blocks[own_lists, :, own_heads[:, None]]
            picked_values = value_blocks[own_lists, :, own_heads[:, None]]
            scores = (
                jnp.einsum(
                    "rhd,hscd->hrsc",
                    query_block[:, first : first + per_group],
                    picked_keys,
                    preferred_element_type=jnp.float32,
                )
                * score_scale
            )
            key_position = (
                own_lists[:, :, None] * tokens_block
                + jnp.arange(tokens_block, dtype=jnp.int32)[None, None, :]
            )
            query_position = cache_len + offset + jnp.arange(tokens_block, dtype=jnp.int32)
            allowed = key_position[:, None, :, :] <= query_position[None, :, None, None]
            scores = jnp.where(allowed, scores, -jnp.inf)
            row_max = jnp.max(scores, axis=(2, 3), keepdims=True)
            powers = jnp.exp(scores - row_max)
            weights = (powers / jnp.sum(powers, axis=(2, 3), keepdims=True)).astype(jnp.bfloat16)
            mixed_rows = jnp.einsum(
                "hrsc,hscd->rhd", weights, picked_values, preferred_element_type=jnp.float32
            )
            pieces.append(mixed_rows.astype(jnp.bfloat16))
        return jnp.concatenate(pieces, axis=1)

    return lax.map(one_block, (query_blocks, block_list, offsets))


def shards(queries, span_keys, span_values, cache_keys, cache_values, block_lists):
    seq_devices = lax.axis_size("seq")
    cache_len = cache_keys.shape[0] * seq_devices
    cache_k, cache_v, fresh_k, fresh_v = (
        lax.all_gather(cache_keys, "seq", axis=0, tiled=True),
        lax.all_gather(cache_values, "seq", axis=0, tiled=True),
        lax.all_gather(span_keys, "seq", axis=0, tiled=True),
        lax.all_gather(span_values, "seq", axis=0, tiled=True),
    )
    key_blocks = jnp.concatenate([cache_k, fresh_k], axis=0).reshape(-1, BLK, KVH, DH)
    value_blocks = jnp.concatenate([cache_v, fresh_v], axis=0).reshape(-1, BLK, KVH, DH)
    kv_of_head = jnp.arange(QUERY_HEADS_HALF, dtype=jnp.int32) // (QUERY_HEADS_HALF // KVH)
    query_blocks = queries.reshape(-1, BLK, QUERY_HEADS_HALF, DH)
    local_blocks = query_blocks.shape[0]
    offsets = (
        lax.axis_index("seq") * local_blocks + jnp.arange(local_blocks, dtype=jnp.int32)
    ) * BLK
    result = attend(
        query_blocks,
        block_lists,
        offsets,
        key_blocks,
        value_blocks,
        kv_of_head,
        QUERY_HEADS_HALF // KVH,
        cache_len,
    )
    return result.reshape(-1, QUERY_HEADS_HALF * DH)


def solution(mesh):
    placed = (
        P(("req", "seq"), None),
        P(("req", "seq"), None),
        P(("req", "seq"), None),
        P(("req", "seq"), None),
        P(("req", "seq"), None),
        P(("req", "seq"), None, None),
    )
    return jax.shard_map(
        shards, mesh=mesh, in_specs=placed, out_specs=P(("req", "seq"), None), check_vma=False
    )
```

profile of v0, /device:TPU:1, one launch (start us, length us, event | category | flops | bytes accessed | tf_op | source)
XLA Modules:
  0.0 252.1 jit_solution(3096035804975677980)
XLA Ops:
  9.4 0.9 fusion.14
  10.5 1.6 copy.56
  13.3 45.3 %all-gather.7.cloned.1.call-done = bf16[2048,512]{1,0:T(8,128)(2,1)} async-done(((bf16[128,512]{1,0:T(8,128)(2,1)}), bf16[2048,512]{1,0:T(8,128)(2,1)}) %all-gather.7.cloned.1.call-update) | async-done | bytes 2097168 | tf_op jit(solution)/shard_map/all_gather | solution.py:65
  58.6 43.4 %all-gather.5.cloned.1.call-done = bf16[2048,512]{1,0:T(8,128)(2,1)} async-done(((bf16[128,512]{1,0:T(8,128)(2,1)}), bf16[2048,512]{1,0:T(8,128)(2,1)}) %all-gather.5.cloned.1.call-update) | async-done | bytes 2097168 | tf_op jit(solution)/shard_map/all_gather | solution.py:63
  102.0 4.4 %pad_maximum_fusion = bf16[4096,512]{1,0:T(8,128)(2,1)} fusion(bf16[2048,512]{1,0:T(8,128)(2,1)} %all-gather.7.cloned.1.call-done, bf16[2048,512]{1,0:T(8,128)(2,1)} %all-gather.5.cloned.1.call-done), kind=kLoop, calls=%fused_computation.8 | loop fusion | flops 8388608 | bytes 8388608 | tf_op jit(solution)/shard_map/concatenate | solution.py:68
  106.5 6.9 %reshape.278 = bf16[32,128,4,128]{3,2,1,0:T(4,128)(2,1)} reshape(bf16[4096,512]{1,0:T(8,128)(2,1)} %pad_maximum_fusion) | data formatting | bytes 8388608 | tf_op jit(solution)/shard_map/reshape | solution.py:68
  113.4 5.3 %copy.52 = bf16[32,128,4,128]{3,1,2,0:T(8,128)(2,1)} copy(bf16[32,128,4,128]{3,2,1,0:T(4,128)(2,1)} %reshape.278) | data formatting | bytes 8388608 | tf_op jit(solution)/shard_map/reshape | solution.py:68
  118.7 26.8 %all-gather.11.cloned.1.call-done = bf16[2048,512]{1,0:T(8,128)(2,1)} async-done(((bf16[128,512]{1,0:T(8,128)(2,1)}), bf16[2048,512]{1,0:T(8,128)(2,1)}) %all-gather.11.cloned.1.call-update) | async-done | bytes 2097168 | tf_op jit(solution)/shard_map/all_gather | solution.py:64
  145.5 43.3 %all-gather.9.cloned.1.call-done = bf16[2048,512]{1,0:T(8,128)(2,1)} async-done(((bf16[128,512]{1,0:T(8,128)(2,1)}), bf16[2048,512]{1,0:T(8,128)(2,1)}) %all-gather.9.cloned.1.call-update) | async-done | bytes 2097168 | tf_op jit(solution)/shard_map/all_gather | solution.py:62
  188.7 4.5 %pad_maximum_fusion.1 = bf16[4096,512]{1,0:T(8,128)(2,1)} fusion(bf16[2048,512]{1,0:T(8,128)(2,1)} %all-gather.11.cloned.1.call-done, bf16[2048,512]{1,0:T(8,128)(2,1)} %all-gather.9.cloned.1.call-done), kind=kLoop, calls=%fused_computation.9 | loop fusion | flops 8388608 | bytes 8388608 | tf_op jit(solution)/shard_map/concatenate | solution.py:67
  193.2 6.9 %reshape.279 = bf16[32,128,4,128]{3,2,1,0:T(4,128)(2,1)} reshape(bf16[4096,512]{1,0:T(8,128)(2,1)} %pad_maximum_fusion.1) | data formatting | bytes 8388608 | tf_op jit(solution)/shard_map/reshape | solution.py:67
  200.1 5.3 %copy.55 = bf16[32,128,4,128]{3,1,2,0:T(8,128)(2,1)} copy(bf16[32,128,4,128]{3,2,1,0:T(4,128)(2,1)} %reshape.279) | data formatting | bytes 8388608 | tf_op jit(solution)/shard_map/reshape | solution.py:67
  205.4 3.8 %gather_fusion.6 = bf16[32,128,128]{2,1,0:T(8,128)(2,1)} fusion(bf16[32,128,4,128]{3,1,2,0:T(8,128)(2,1)} %copy.52, s32[32]{0:T(128)S(1)} %reshape.258), kind=kCustom, calls=%fused_computation.6 | custom fusion | bytes 2097408 | tf_op jit(solution)/shard_map/while/body/eval_jaxpr/gather | solution.py:29
  209.3 3.8 %gather_fusion.7 = bf16[32,128,128]{2,1,0:T(8,128)(2,1)} fusion(bf16[32,128,4,128]{3,1,2,0:T(8,128)(2,1)} %copy.55, s32[32]{0:T(128)S(1)} %reshape.258), kind=kCustom, calls=%fused_computation.7 | custom fusion | bytes 2097408 | tf_op jit(solution)/shard_map/while/body/eval_jaxpr/gather | solution.py:28
  213.1 3.9 %gather_fusion.4 = bf16[32,128,128]{2,1,0:T(8,128)(2,1)} fusion(bf16[32,128,4,128]{3,1,2,0:T(8,128)(2,1)} %copy.52, s32[32]{0:T(128)S(1)} %reshape.246), kind=kCustom, calls=%fused_computation.4 | custom fusion | bytes 2097408 | tf_op jit(solution)/shard_map/while/body/eval_jaxpr/gather | solution.py:29
  217.0 3.8 %gather_fusion.5 = bf16[32,128,128]{2,1,0:T(8,128)(2,1)} fusion(bf16[32,128,4,128]{3,1,2,0:T(8,128)(2,1)} %copy.55, s32[32]{0:T(128)S(1)} %reshape.246), kind=kCustom, calls=%fused_computation.5 | custom fusion | bytes 2097408 | tf_op jit(solution)/shard_map/while/body/eval_jaxpr/gather | solution.py:28
  220.9 3.8 %gather_fusion.2 = bf16[32,128,128]{2,1,0:T(8,128)(2,1)} fusion(bf16[32,128,4,128]{3,1,2,0:T(8,128)(2,1)} %copy.52, s32[32]{0:T(128)S(1)} %reshape.234), kind=kCustom, calls=%fused_computation.2 | custom fusion | bytes 2097408 | tf_op jit(solution)/shard_map/while/body/eval_jaxpr/gather | solution.py:29
  224.7 3.9 %gather_fusion.3 = bf16[32,128,128]{2,1,0:T(8,128)(2,1)} fusion(bf16[32,128,4,128]{3,1,2,0:T(8,128)(2,1)} %copy.55, s32[32]{0:T(128)S(1)} %reshape.234), kind=kCustom, calls=%fused_computation.3 | custom fusion | bytes 2097408 | tf_op jit(solution)/shard_map/while/body/eval_jaxpr/gather | solution.py:28
  228.6 2.9 %gather_fusion = bf16[32,128,128]{2,1,0:T(8,128)(2,1)S(1)} fusion(bf16[32,128,4,128]{3,1,2,0:T(8,128)(2,1)} %copy.52, s32[32]{0:T(128)S(1)} %reshape.222), kind=kCustom, calls=%fused_computation | custom fusion | bytes 2097408 | tf_op jit(solution)/shard_map/while/body/eval_jaxpr/gather | solution.py:29
  231.6 2.9 %gather_fusion.1 = bf16[32,128,128]{2,1,0:T(8,128)(2,1)S(1)} fusion(bf16[32,128,4,128]{3,1,2,0:T(8,128)(2,1)} %copy.55, s32[32]{0:T(128)S(1)} %reshape.222), kind=kCustom, calls=%fused_computation.1 | custom fusion | bytes 2097408 | tf_op jit(solution)/shard_map/while/body/eval_jaxpr/gather | solution.py:28
  234.5 1.9 fusion.32
  238.0 0.8 fusion.33
  240.4 0.8 fusion.34
  244.3 1.3 copy.81
  (50 shorter events, 10.3 us)
Async XLA Ops:
  6.5 5.6 %copy-start.5 = (s32[1,32,4]{1,2,0:T(4,128)S(1)}, s32[1,32,4]{1,2,0:T(4,128)}, u32[]{:S(2)}) copy-start(s32[1,32,4]{1,2,0:T(4,128)} %param.11) | copy-start | bytes 1540
  6.5 52.1 %all-gather.7.cloned.1.call-start = ((), (), s32[]{:S(2)}) async-start(), calls=%async_computation.1 | async-start | bytes 2228224 | tf_op jit(solution)/shard_map/all_gather | solution.py:65
  7.3 94.8 %all-gather.5.cloned.1.call-start = ((), (), s32[]{:S(2)}) async-start(), calls=%async_computation | async-start | bytes 2228224 | tf_op jit(solution)/shard_map/all_gather | solution.py:63
  8.0 137.5 %all-gather.11.cloned.1.call-start = ((), (), s32[]{:S(2)}) async-start(), calls=%async_computation.3 | async-start | bytes 2228224 | tf_op jit(solution)/shard_map/all_gather | solution.py:64
  8.7 180.0 %all-gather.9.cloned.1.call-start = ((), (), s32[]{:S(2)}) async-start(), calls=%async_computation.2 | async-start | bytes 2228224 | tf_op jit(solution)/shard_map/all_gather | solution.py:62
  234.5 2.2 copy-start.4
  236.7 1.2 copy-start.3
  238.0 1.2 copy-start.2
  239.2 1.2 copy-start.1
  240.4 1.2 copy-start
Sparse Core Ops, SparseCore 0:
  9.5 49.0 all-gather.6
  60.7 41.2 all-gather.4
  104.2 41.2 all-gather.10
  147.4 41.2 all-gather.8
where the time goes:
time: 253 us; the launch traced here: 252 us
  waiting for transfers between devices  161 us (64%)
  local copies, waits for them, and re-layouts  58.7 us (23%)
  between operations  13.3 us (5%)
  other arithmetic  11.5 us (5%)
  matrix products  7.04 us (3%)
    all_gather x1, waiting for transfers between devices, shards(): lax.all_gather(span_values, 'seq', axis=0, tiled=True)  45.3 us
    all_gather x1, waiting for transfers between devices, shards(): lax.all_gather(cache_values, 'seq', axis=0, tiled=True)  43.4 us
    all_gather x1, waiting for transfers between devices, shards(): lax.all_gather(cache_keys, 'seq', axis=0, tiled=True)  43.3 us
    all_gather x1, waiting for transfers between devices, shards(): lax.all_gather(span_keys, 'seq', axis=0, tiled=True)  26.8 us
    gather x4, local copies, waits for them, and re-layouts, one_block(): picked_values = value_blocks[own_lists, :, own_heads[:, None]]  14.5 us
    gather x4, local copies, waits for them, and re-layouts, one_block(): picked_keys = key_blocks[own_lists, :, own_heads[:, None]]  14.5 us
    reshape x2, local copies, waits for them, and re-layouts, shards(): jnp.concatenate([cache_k, fresh_k], axis=0).reshape(-1, BLK, KVH, DH)  12.2 us
    reshape x2, local copies, waits for them, and re-layouts, shards(): jnp.concatenate([cache_v, fresh_v], axis=0).reshape(-1, BLK, KVH, DH)  12.2 us
  transfers between devices with their start and end apart: 4, of which 4 were waited for; matrix products, arithmetic and copies ran while one was open for 8% of the time, Pallas kernels for 0%

commit v1 on v0

v1 whole, which is shorter than its diff:
```python
import math

import jax
import jax.numpy as jnp
import numpy as np
from jax import lax
from jax.experimental import pallas as pl
from jax.experimental.pallas import tpu as pltpu
from jax.sharding import PartitionSpec as P

HEADS = 32
KVH = 4
GROUP = HEADS // KVH
DH = 128
BLK = 128
WIDTH = KVH * DH
SEQ = 16
CHIPS = SEQ // 2
SCALE = math.log2(math.e) / math.sqrt(DH)

RING = [(2 * z, 2 * ((z + 1) % CHIPS)) for z in range(CHIPS)] + [
    (2 * z + 1, 2 * ((z - 1) % CHIPS) + 1) for z in range(CHIPS)
]
SWAP = [(i, i ^ 1) for i in range(SEQ)]

NAMES = ["own", "oth"] + [
    kind + str(step) + lane
    for step in (1, 2, 3, 4)
    for lane in ("A", "B")
    for kind in ("got", "swp")
    if (step, lane) != (4, "B")
]


def slot_table():
    table = np.zeros((2, CHIPS, 2), np.int32)
    for core in range(2):
        for away in range(CHIPS):
            for owner in range(2):
                if away == 0:
                    name = "own" if owner == core else "oth"
                else:
                    down = away < 4 or (away == 4 and owner == 1)
                    step = away if down else CHIPS - away
                    lane = "A" if owner == (1 if down else 0) else "B"
                    kind = "got" if core == (1 if down else 0) else "swp"
                    name = kind + str(step) + lane
                table[core, away, owner] = NAMES.index(name)
    return table


def pick(slot, low, high, use):
    if high - low == 1:
        use(low)
        return
    middle = (low + high) // 2

    @pl.when(slot < middle)
    def _():
        pick(slot, low, middle, use)

    @pl.when(slot >= middle)
    def _():
        pick(slot, middle, high, use)


def attend_kernel(slot_ref, half_ref, q_ref, *refs):
    held = refs[: len(NAMES)]
    o_ref, k_fix, v_fix, k_pick, v_pick, fix_sem, pick_sem = refs[len(NAMES) :]

    def fix_copies(n, buffer, half):
        column = pl.multiple_of(half * 2 * WIDTH, 2 * WIDTH)
        return (
            pltpu.make_async_copy(held[buffer].at[:, pl.ds(column, WIDTH)], k_fix.at[n], fix_sem.at[n, 0]),
            pltpu.make_async_copy(held[buffer].at[:, pl.ds(column + WIDTH, WIDTH)], v_fix.at[n], fix_sem.at[n, 1]),
        )

    def pick_copies(h, buffer, half):
        column = pl.multiple_of(half * 2 * WIDTH + (h // GROUP) * DH, DH)
        return (
            pltpu.make_async_copy(held[buffer].at[:, pl.ds(column, DH)], k_pick.at[h], pick_sem.at[h, 0]),
            pltpu.make_async_copy(held[buffer].at[:, pl.ds(column + WIDTH, DH)], v_pick.at[h], pick_sem.at[h, 1]),
        )

    def start(copies):
        for copy in copies:
            copy.start()

    start(fix_copies(2, 0, 1))
    for n in range(2):
        pick(slot_ref[HEADS + n], 0, len(NAMES), lambda b: start(fix_copies(n, b, half_ref[HEADS + n])))

    def start_head(h, carry):
        pick(slot_ref[h], 0, len(NAMES), lambda b: start(pick_copies(h, b, half_ref[h])))
        return carry

    lax.fori_loop(0, HEADS, start_head, 0)

    for n in range(3):
        for copy in fix_copies(n, 0, 0):
            copy.wait()
    row = lax.broadcasted_iota(jnp.int32, (BLK, BLK), 0)
    col = lax.broadcasted_iota(jnp.int32, (BLK, BLK), 1)
    seen = col <= row
    over_rows = (((1,), (1,)), ((), ()))
    over_keys = (((1,), (0,)), ((), ()))
    for g in range(KVH):
        cols = slice(g * DH, (g + 1) * DH)
        keys = jnp.concatenate([k_fix[n, :, cols] for n in range(3)], axis=0)
        values = jnp.concatenate([v_fix[n, :, cols] for n in range(3)], axis=0)
        heads = range(g * GROUP, (g + 1) * GROUP)
        queries = jnp.concatenate([q_ref[:, h * DH : (h + 1) * DH] for h in heads], axis=0)
        fixed = lax.dot_general(queries, keys, over_rows, preferred_element_type=jnp.float32)
        for h in heads:
            for copy in pick_copies(h, 0, 0):
                copy.wait()
        powers_fixed, powers_picked, sums = [], [], []
        for n, h in enumerate(heads):
            part = fixed[n * BLK : (n + 1) * BLK]
            old = part[:, : 2 * BLK]
            new = jnp.where(seen, part[:, 2 * BLK :], -jnp.inf)
            picked = lax.dot_general(
                q_ref[:, h * DH : (h + 1) * DH], k_pick[h], over_rows, preferred_element_type=jnp.float32
            )
            scores = jnp.concatenate([old, new, picked], axis=1)
            top = jnp.max(scores, axis=1, keepdims=True)
            powers = jnp.exp2((scores - top) * SCALE)
            sums.append(jnp.sum(powers, axis=1, keepdims=True))
            powers = powers.astype(jnp.bfloat16)
            powers_fixed.append(powers[:, : 3 * BLK])
            powers_picked.append(powers[:, 3 * BLK :])
        mixed = lax.dot_general(
            jnp.concatenate(powers_fixed, axis=0), values, over_keys, preferred_element_type=jnp.float32
        )
        for n, h in enumerate(heads):
            total = mixed[n * BLK : (n + 1) * BLK] + lax.dot_general(
                powers_picked[n], v_pick[h], over_keys, preferred_element_type=jnp.float32
            )
            o_ref[:, h * DH : (h + 1) * DH] = (total / sums[n]).astype(jnp.bfloat16)


def attend(slots, halves, queries, held):
    return pl.pallas_call(
        attend_kernel,
        out_shape=jax.ShapeDtypeStruct((BLK, HEADS * DH), jnp.bfloat16),
        in_specs=[pl.BlockSpec(memory_space=pltpu.SMEM)] * 2
        + [pl.BlockSpec(memory_space=pltpu.VMEM)]
        + [pl.BlockSpec(memory_space=pl.ANY)] * len(NAMES),
        out_specs=pl.BlockSpec(memory_space=pltpu.VMEM),
        scratch_shapes=[
            pltpu.VMEM((3, BLK, WIDTH), jnp.bfloat16),
            pltpu.VMEM((3, BLK, WIDTH), jnp.bfloat16),
            pltpu.VMEM((HEADS, BLK, DH), jnp.bfloat16),
            pltpu.VMEM((HEADS, BLK, DH), jnp.bfloat16),
            pltpu.SemaphoreType.DMA((3, 2)),
            pltpu.SemaphoreType.DMA((HEADS, 2)),
        ],
        compiler_params=pltpu.CompilerParams(vmem_limit_bytes=32 * 1024 * 1024),
        cost_estimate=pl.CostEstimate(flops=1 << 30, bytes_accessed=6 << 20, transcendentals=1 << 21),
    )(slots, halves, queries, *held)


def shards(queries, span_keys, span_values, cache_keys, cache_values, block_lists):
    me = lax.axis_index("seq")
    own = jnp.concatenate([cache_keys, cache_values, span_keys, span_values], axis=1)
    held = {"own": own, "oth": lax.ppermute(own, "seq", SWAP)}
    last = {"A": held["own"], "B": held["oth"]}
    for step in (1, 2, 3, 4):
        for lane in ("A", "B"):
            if (step, lane) == (4, "B"):
                continue
            last[lane] = lax.ppermute(last[lane], "seq", RING)
            held["got" + str(step) + lane] = last[lane]
            held["swp" + str(step) + lane] = lax.ppermute(last[lane], "seq", SWAP)

    lists = block_lists.reshape(HEADS, 4)
    chosen = jnp.sum(lists, axis=1) - (2 * (SEQ + me) - 1)
    blocks = jnp.concatenate([chosen, jnp.zeros((1,), jnp.int32), (SEQ + me - 1).reshape(1)]).astype(jnp.int32)
    blocks = jnp.clip(blocks, 0, 2 * SEQ - 1)
    owner = blocks % SEQ
    away = (owner // 2 - me // 2) % CHIPS
    table = jnp.asarray(slot_table().reshape(-1))
    slots = table[(me % 2) * 2 * CHIPS + away * 2 + owner % 2]
    return attend(slots, blocks // SEQ, queries, [held[name] for name in NAMES])


def solution(mesh):
    rows = P(("req", "seq"), None)
    return jax.shard_map(
        shards,
        mesh=mesh,
        in_specs=(rows,) * 5 + (P(("req", "seq"), None, None),),
        out_specs=rows,
        check_vma=False,
    )
```

time: 253 us -> 80.4 us (0.32)
  waiting for transfers between devices: 161 us -> 9.77 us
  starting transfers between devices: 0.12 us -> 54.5 us
  local copies, waits for them, and re-layouts: 58.7 us -> 6.26 us
  between operations: 13.3 us -> 0.29 us
  other arithmetic: 11.5 us -> 0.23 us
  Pallas kernels: 0 us -> 8.75 us
  matrix products: 7.04 us -> 0 us
    all_gather x4 -> x0, waiting for transfers between devices: 159 us -> none  [the longest x1 45.3 us: shards(): lax.all_gather(span_values, 'seq', axis=0, tiled=True)]
    ppermute x0 -> x15, starting transfers between devices: none -> 54.5 us  [the longest x7 35.4 us: shards(): last[lane] = lax.ppermute(last[lane], 'seq', RING)]
    gather x8 -> x1, local copies, waits for them, and re-layouts: 29 us -> 0.78 us  [shards(): slots = table[me % 2 * 2 * CHIPS + away * 2 + owner % 2]]
    reshape x5 -> x0, local copies, waits for them, and re-layouts: 25.8 us -> none  [the longest x2 12.2 us: shards(): jnp.concatenate([cache_k, fresh_k], axis=0).reshape(-1, BLK, KVH, DH)]
    concatenate x5 -> x1, other arithmetic: 10 us -> 0.01 us  [shards(): jnp.concatenate([chosen, jnp.zeros((1,), jnp.int32), (SEQ + me - 1).resha...]
    ppermute x0 -> x15, waiting for transfers between devices: none -> 9.77 us  [the longest x7 8.95 us: shards(): last[lane] = lax.ppermute(last[lane], 'seq', RING)]
    pallas_call x0 -> x1, Pallas kernels: none -> 8.75 us  [attend(): pl.pallas_call(attend_kernel, out_shape=jax.ShapeDtypeStruct((BLK, HEADS...]
    dot_general x8 -> x0, matrix products: 7.04 us -> none  [the longest x4 4.25 us: one_block(): jnp.einsum('rhd,hscd->hrsc', query_block[:, first:first + per_group], pic...]
  transfers between devices with their start and end apart: 4 -> 15, of which waited for: 4 -> 4; matrix products, arithmetic and copies ran while one was open for 8% -> 1% of each run, Pallas kernels for 0% -> 0%
where the time goes in v1:
time: 80.4 us; the launch traced here: 79.8 us
  starting transfers between devices  54.5 us (68%)
  waiting for transfers between devices  9.77 us (12%)
  Pallas kernels  8.75 us (11%)
  local copies, waits for them, and re-layouts  6.26 us (8%)
    ppermute x7, starting transfers between devices, shards(): last[lane] = lax.ppermute(last[lane], 'seq', RING)  35.4 us
    ppermute x7, starting transfers between devices, shards(): held['swp' + str(step) + lane] = lax.ppermute(last[lane], 'seq', SWAP)  17.2 us
    ppermute x7, waiting for transfers between devices, shards(): last[lane] = lax.ppermute(last[lane], 'seq', RING)  8.95 us
    pallas_call x1, Pallas kernels, attend(): pl.pallas_call(attend_kernel, out_shape=jax.ShapeDtypeStruct((BLK, HEADS...  8.75 us
    unnamed x13, local copies, waits for them, and re-layouts  4.56 us
    ppermute x1, starting transfers between devices, shards(): held = {'own': own, 'oth': lax.ppermute(own, 'seq', SWAP)}  1.92 us
  transfers between devices with their start and end apart: 15, of which 4 were waited for; matrix products, arithmetic and copies ran while one was open for 1% of the time, Pallas kernels for 0%

profile of v1, /device:TPU:1, one launch (start us, length us, event | category | flops | bytes accessed | tf_op | source)
XLA Modules:
  0.0 79.8 jit_solution(11188838987536540508)
XLA Ops:
  0.0 1.0 %constant_dynamic-update-slice_fusion.3 = bf16[128,2048]{1,0:T(8,128)(2,1)S(1)} fusion(bf16[128,512]{1,0:T(8,128)(2,1)} %param.10), kind=kLoop, calls=%fused_computation.4 | loop fusion | bytes 262144
  1.0 0.9 %constant_dynamic-update-slice_fusion.2 = bf16[128,2048]{1,0:T(8,128)(2,1)S(1)} fusion(bf16[128,2048]{1,0:T(8,128)(2,1)S(1)} %constant_dynamic-update-slice_fusion.3, bf16[128,512]{1,0:T(8,128)(2,1)} %param.11), kind=kLoop, calls=%fused_computation.3 | loop fusion | bytes 262144
  1.9 0.9 %constant_dynamic-update-slice_fusion.1 = bf16[128,2048]{1,0:T(8,128)(2,1)S(1)} fusion(bf16[128,2048]{1,0:T(8,128)(2,1)S(1)} %constant_dynamic-update-slice_fusion.2, bf16[128,512]{1,0:T(8,128)(2,1)} %param.8), kind=kLoop, calls=%fused_computation.2 | loop fusion | bytes 262144
  2.8 0.9 %constant_dynamic-update-slice_fusion.refs_0_ = bf16[128,2048]{1,0:T(8,128)(2,1)S(1)} fusion(bf16[128,2048]{1,0:T(8,128)(2,1)S(1)} %constant_dynamic-update-slice_fusion.1, bf16[128,512]{1,0:T(8,128)(2,1)} %param.9), kind=kLoop, calls=%fused_computation.1 | loop fusion | bytes 262144 | tf_op jit(solution)/shard_map/concatenate | solution.py:165
  3.8 11.5 %collective-permute-start.1 = (bf16[128,2048]{1,0:T(8,128)(2,1)S(1)}, bf16[128,2048]{1,0:T(8,128)(2,1)S(1)}, u32[]{:S(2)}, u32[]{:S(2)}) collective-permute-start(bf16[128,2048]{1,0:T(8,128)(2,1)S(1)} %constant_dynamic-update-slice_fusion.refs_0_), channel_id=1, source_target_pairs={{0,2},{2,4},{4,6},{6,8},{8,10},{10,12},{12,14},{14,0},{1,15},{3,1}... | collective-permute-start | bytes 1572872 | tf_op jit(solution)/shard_map/ppermute | solution.py:172
  15.3 1.9 %collective-permute-start = (bf16[128,2048]{1,0:T(8,128)(2,1)S(1)}, bf16[128,2048]{1,0:T(8,128)(2,1)S(1)}, u32[]{:S(2)}, u32[]{:S(2)}) collective-permute-start(bf16[128,2048]{1,0:T(8,128)(2,1)S(1)} %constant_dynamic-update-slice_fusion.refs_0_), channel_id=1, source_target_pairs={{0,1},{1,0},{2,3},{3,2},{4,5},{5,4},{6,7},{7,6},{8,9},{9,8},{10,11... | collective-permute-start | bytes 1572872 | tf_op jit(solution)/shard_map/ppermute | solution.py:166
  17.2 4.2 %collective-permute-done.1.refs_2_ = bf16[128,2048]{1,0:T(8,128)(2,1)S(1)} collective-permute-done((bf16[128,2048]{1,0:T(8,128)(2,1)S(1)}, bf16[128,2048]{1,0:T(8,128)(2,1)S(1)}, u32[]{:S(2)}, u32[]{:S(2)}) %collective-permute-start.1) | collective-permute-done | bytes 524320 | tf_op jit(solution)/shard_map/ppermute | solution.py:172
  21.4 5.0 %collective-permute-start.5 = (bf16[128,2048]{1,0:T(8,128)(2,1)S(1)}, bf16[128,2048]{1,0:T(8,128)(2,1)S(1)}, u32[]{:S(2)}, u32[]{:S(2)}) collective-permute-start(bf16[128,2048]{1,0:T(8,128)(2,1)S(1)} %collective-permute-done.1.refs_2_), channel_id=1, source_target_pairs={{0,2},{2,4},{4,6},{6,8},{8,10},{10,12},{12,14},{14,0},{1,15},{3,1}... | collective-permute-start | bytes 1572872 | tf_op jit(solution)/shard_map/ppermute | solution.py:172
  26.4 1.9 %collective-permute-start.3 = (bf16[128,2048]{1,0:T(8,128)(2,1)S(1)}, bf16[128,2048]{1,0:T(8,128)(2,1)S(1)}, u32[]{:S(2)}, u32[]{:S(2)}) collective-permute-start(bf16[128,2048]{1,0:T(8,128)(2,1)S(1)} %collective-permute-done.refs_1_), channel_id=1, source_target_pairs={{0,2},{2,4},{4,6},{6,8},{8,10},{10,12},{12,14},{14,0},{1,15},{3,1}... | collective-permute-start | bytes 1572872 | tf_op jit(solution)/shard_map/ppermute | solution.py:172
  28.3 4.2 %collective-permute-done.5.refs_6_ = bf16[128,2048]{1,0:T(8,128)(2,1)S(1)} collective-permute-done((bf16[128,2048]{1,0:T(8,128)(2,1)S(1)}, bf16[128,2048]{1,0:T(8,128)(2,1)S(1)}, u32[]{:S(2)}, u32[]{:S(2)}) %collective-permute-start.5) | collective-permute-done | bytes 524320 | tf_op jit(solution)/shard_map/ppermute | solution.py:172
  32.5 5.0 %collective-permute-start.9 = (bf16[128,2048]{1,0:T(8,128)(2,1)S(1)}, bf16[128,2048]{1,0:T(8,128)(2,1)}, u32[]{:S(2)}, u32[]{:S(2)}) collective-permute-start(bf16[128,2048]{1,0:T(8,128)(2,1)S(1)} %collective-permute-done.5.refs_6_), channel_id=1, source_target_pairs={{0,2},{2,4},{4,6},{6,8},{8,10},{10,12},{12,14},{14,0},{1,15},{3,1}... | collective-permute-start | bytes 1572872 | tf_op jit(solution)/shard_map/ppermute | solution.py:172
  38.1 5.0 %collective-permute-start.7 = (bf16[128,2048]{1,0:T(8,128)(2,1)S(1)}, bf16[128,2048]{1,0:T(8,128)(2,1)}, u32[]{:S(2)}, u32[]{:S(2)}) collective-permute-start(bf16[128,2048]{1,0:T(8,128)(2,1)S(1)} %collective-permute-done.3.refs_4_), channel_id=1, source_target_pairs={{0,2},{2,4},{4,6},{6,8},{8,10},{10,12},{12,14},{14,0},{1,15},{3,1}... | collective-permute-start | bytes 1572872 | tf_op jit(solution)/shard_map/ppermute | solution.py:172
  43.1 2.0 %collective-permute-start.2 = (bf16[128,2048]{1,0:T(8,128)(2,1)S(1)}, bf16[128,2048]{1,0:T(8,128)(2,1)}, u32[]{:S(2)}, u32[]{:S(2)}) collective-permute-start(bf16[128,2048]{1,0:T(8,128)(2,1)S(1)} %collective-permute-done.1.refs_2_), channel_id=1, source_target_pairs={{0,1},{1,0},{2,3},{3,2},{4,5},{5,4},{6,7},{7,6},{8,9},{9,8},{10,11... | collective-permute-start | bytes 1572872 | tf_op jit(solution)/shard_map/ppermute | solution.py:174
  45.1 2.4 %collective-permute-start.6 = (bf16[128,2048]{1,0:T(8,128)(2,1)S(1)}, bf16[128,2048]{1,0:T(8,128)(2,1)}, u32[]{:S(2)}, u32[]{:S(2)}) collective-permute-start(bf16[128,2048]{1,0:T(8,128)(2,1)S(1)} %collective-permute-done.5.refs_6_), channel_id=1, source_target_pairs={{0,1},{1,0},{2,3},{3,2},{4,5},{5,4},{6,7},{7,6},{8,9},{9,8},{10,11... | collective-permute-start | bytes 1572872 | tf_op jit(solution)/shard_map/ppermute | solution.py:174
  47.5 4.4 %collective-permute-start.13 = (bf16[128,2048]{1,0:T(8,128)(2,1)}, bf16[128,2048]{1,0:T(8,128)(2,1)}, u32[]{:S(2)}, u32[]{:S(2)}) collective-permute-start(bf16[128,2048]{1,0:T(8,128)(2,1)} %collective-permute-done.9.refs_10_), channel_id=1, source_target_pairs={{0,2},{2,4},{4,6},{6,8},{8,10},{10,12},{12,14},{14,0},{1,15},{3,1}... | collective-permute-start | bytes 1572872 | tf_op jit(solution)/shard_map/ppermute | solution.py:172
  51.9 2.5 %collective-permute-start.11 = (bf16[128,2048]{1,0:T(8,128)(2,1)}, bf16[128,2048]{1,0:T(8,128)(2,1)}, u32[]{:S(2)}, u32[]{:S(2)}) collective-permute-start(bf16[128,2048]{1,0:T(8,128)(2,1)} %collective-permute-done.7.refs_8_), channel_id=1, source_target_pairs={{0,2},{2,4},{4,6},{6,8},{8,10},{10,12},{12,14},{14,0},{1,15},{3,1}... | collective-permute-start | bytes 1572872 | tf_op jit(solution)/shard_map/ppermute | solution.py:172
  55.2 3.0 %collective-permute-start.4 = (bf16[128,2048]{1,0:T(8,128)(2,1)}, bf16[128,2048]{1,0:T(8,128)(2,1)}, u32[]{:S(2)}, u32[]{:S(2)}) collective-permute-start(bf16[128,2048]{1,0:T(8,128)(2,1)} %copy-done.1), channel_id=1, source_target_pairs={{0,1},{1,0},{2,3},{3,2},{4,5},{5,4},{6,7},{7,6},{8,9},{9,8},{10,11... | collective-permute-start | bytes 1572872 | tf_op jit(solution)/shard_map/ppermute | solution.py:174
  58.2 1.9 %collective-permute-start.10 = (bf16[128,2048]{1,0:T(8,128)(2,1)}, bf16[128,2048]{1,0:T(8,128)(2,1)}, u32[]{:S(2)}, u32[]{:S(2)}) collective-permute-start(bf16[128,2048]{1,0:T(8,128)(2,1)} %collective-permute-done.9.refs_10_), channel_id=1, source_target_pairs={{0,1},{1,0},{2,3},{3,2},{4,5},{5,4},{6,7},{7,6},{8,9},{9,8},{10,11... | collective-permute-start | bytes 1572872 | tf_op jit(solution)/shard_map/ppermute | solution.py:174
  60.2 2.4 %collective-permute-start.8 = (bf16[128,2048]{1,0:T(8,128)(2,1)}, bf16[128,2048]{1,0:T(8,128)(2,1)}, u32[]{:S(2)}, u32[]{:S(2)}) collective-permute-start(bf16[128,2048]{1,0:T(8,128)(2,1)} %collective-permute-done.7.refs_8_), channel_id=1, source_target_pairs={{0,1},{1,0},{2,3},{3,2},{4,5},{5,4},{6,7},{7,6},{8,9},{9,8},{10,11... | collective-permute-start | bytes 1572872 | tf_op jit(solution)/shard_map/ppermute | solution.py:174
  62.6 1.9 %collective-permute-start.14 = (bf16[128,2048]{1,0:T(8,128)(2,1)}, bf16[128,2048]{1,0:T(8,128)(2,1)}, u32[]{:S(2)}, u32[]{:S(2)}) collective-permute-start(bf16[128,2048]{1,0:T(8,128)(2,1)} %collective-permute-done.13.refs_14_), channel_id=1, source_target_pairs={{0,1},{1,0},{2,3},{3,2},{4,5},{5,4},{6,7},{7,6},{8,9},{9,8},{10,11... | collective-permute-start | bytes 1572872 | tf_op jit(solution)/shard_map/ppermute | solution.py:174
  64.5 3.6 %collective-permute-start.12 = (bf16[128,2048]{1,0:T(8,128)(2,1)}, bf16[128,2048]{1,0:T(8,128)(2,1)}, u32[]{:S(2)}, u32[]{:S(2)}) collective-permute-start(bf16[128,2048]{1,0:T(8,128)(2,1)} %collective-permute-done.11.refs_12_), channel_id=1, source_target_pairs={{0,1},{1,0},{2,3},{3,2},{4,5},{5,4},{6,7},{7,6},{8,9},{9,8},{10,11... | collective-permute-start | bytes 1572872 | tf_op jit(solution)/shard_map/ppermute | solution.py:174
  69.2 0.8 %collective-permute-done.12.refs_13_ = bf16[128,2048]{1,0:T(8,128)(2,1)} collective-permute-done((bf16[128,2048]{1,0:T(8,128)(2,1)}, bf16[128,2048]{1,0:T(8,128)(2,1)}, u32[]{:S(2)}, u32[]{:S(2)}) %collective-permute-start.12) | collective-permute-done | bytes 524320 | tf_op jit(solution)/shard_map/ppermute | solution.py:174
  70.0 1.0 %copy-done.2 = bf16[128,2048]{1,0:T(8,128)(2,1)S(1)} copy-done((bf16[128,2048]{1,0:T(8,128)(2,1)S(1)}, bf16[128,2048]{1,0:T(8,128)(2,1)}, u32[]{:S(2)}) %copy-start.2) | copy-done | bytes 524312
  71.0 8.7 %shard_map.73 = bf16[128,4096]{1,0:T(8,128)(2,1)} custom-call(s32[34]{0:T(128)S(1)} %gather_fusion, s32[34]{0:T(128)S(1)} %and_select_fusion.half_ref, bf16[128,4096]{1,0:T(8,128)(2,1)S(1)} %copy-done, bf16[128,2048]{1,0:T(8,128)(2,1)S(1)} %constant_dynamic-update-slice_fusion.refs_0_, bf16[128,2048]{1,0:T(8,128)(2,1)S(1)} %collective-permute-done.refs_1_, ...), custom_call_target="tpu_custom_call" | custom-call | flops 1073741824 | bytes 6291456 | tf_op jit(solution)/shard_map/pallas_call | solution.py:143
  (28 shorter events, 2.3 us)
Async XLA Ops:
  0.0 70.0 %copy-start = (bf16[128,4096]{1,0:T(8,128)(2,1)S(1)}, bf16[128,4096]{1,0:T(8,128)(2,1)}, u32[]{:S(2)}) copy-start(bf16[128,4096]{1,0:T(8,128)(2,1)} %q_ref.1) | copy-start | bytes 3145732
  3.8 17.6 %collective-permute-start.1 = (bf16[128,2048]{1,0:T(8,128)(2,1)S(1)}, bf16[128,2048]{1,0:T(8,128)(2,1)S(1)}, u32[]{:S(2)}, u32[]{:S(2)}) collective-permute-start(bf16[128,2048]{1,0:T(8,128)(2,1)S(1)} %constant_dynamic-update-slice_fusion.refs_0_), channel_id=1, source_target_pairs={{0,2},{2,4},{4,6},{6,8},{8,10},{10,12},{12,14},{14,0},{1,15},{3,1}... | collective-permute-start | bytes 1572872 | tf_op jit(solution)/shard_map/ppermute | solution.py:172
  15.3 11.1 %collective-permute-start = (bf16[128,2048]{1,0:T(8,128)(2,1)S(1)}, bf16[128,2048]{1,0:T(8,128)(2,1)S(1)}, u32[]{:S(2)}, u32[]{:S(2)}) collective-permute-start(bf16[128,2048]{1,0:T(8,128)(2,1)S(1)} %constant_dynamic-update-slice_fusion.refs_0_), channel_id=1, source_target_pairs={{0,1},{1,0},{2,3},{3,2},{4,5},{5,4},{6,7},{7,6},{8,9},{9,8},{10,11... | collective-permute-start | bytes 1572872 | tf_op jit(solution)/shard_map/ppermute | solution.py:166
  21.4 11.1 %collective-permute-start.5 = (bf16[128,2048]{1,0:T(8,128)(2,1)S(1)}, bf16[128,2048]{1,0:T(8,128)(2,1)S(1)}, u32[]{:S(2)}, u32[]{:S(2)}) collective-permute-start(bf16[128,2048]{1,0:T(8,128)(2,1)S(1)} %collective-permute-done.1.refs_2_), channel_id=1, source_target_pairs={{0,2},{2,4},{4,6},{6,8},{8,10},{10,12},{12,14},{14,0},{1,15},{3,1}... | collective-permute-start | bytes 1572872 | tf_op jit(solution)/shard_map/ppermute | solution.py:172
  26.4 11.7 %collective-permute-start.3 = (bf16[128,2048]{1,0:T(8,128)(2,1)S(1)}, bf16[128,2048]{1,0:T(8,128)(2,1)S(1)}, u32[]{:S(2)}, u32[]{:S(2)}) collective-permute-start(bf16[128,2048]{1,0:T(8,128)(2,1)S(1)} %collective-permute-done.refs_1_), channel_id=1, source_target_pairs={{0,2},{2,4},{4,6},{6,8},{8,10},{10,12},{12,14},{14,0},{1,15},{3,1}... | collective-permute-start | bytes 1572872 | tf_op jit(solution)/shard_map/ppermute | solution.py:172
  32.5 15.0 %collective-permute-start.9 = (bf16[128,2048]{1,0:T(8,128)(2,1)S(1)}, bf16[128,2048]{1,0:T(8,128)(2,1)}, u32[]{:S(2)}, u32[]{:S(2)}) collective-permute-start(bf16[128,2048]{1,0:T(8,128)(2,1)S(1)} %collective-permute-done.5.refs_6_), channel_id=1, source_target_pairs={{0,2},{2,4},{4,6},{6,8},{8,10},{10,12},{12,14},{14,0},{1,15},{3,1}... | collective-permute-start | bytes 1572872 | tf_op jit(solution)/shard_map/ppermute | solution.py:172
  38.1 9.4 %copy-start.1 = (bf16[128,2048]{1,0:T(8,128)(2,1)}, bf16[128,2048]{1,0:T(8,128)(2,1)S(1)}, u32[]{:S(2)}) copy-start(bf16[128,2048]{1,0:T(8,128)(2,1)S(1)} %collective-permute-done.3.refs_4_) | copy-start | bytes 1572868
  38.1 13.8 %collective-permute-start.7 = (bf16[128,2048]{1,0:T(8,128)(2,1)S(1)}, bf16[128,2048]{1,0:T(8,128)(2,1)}, u32[]{:S(2)}, u32[]{:S(2)}) collective-permute-start(bf16[128,2048]{1,0:T(8,128)(2,1)S(1)} %collective-permute-done.3.refs_4_), channel_id=1, source_target_pairs={{0,2},{2,4},{4,6},{6,8},{8,10},{10,12},{12,14},{14,0},{1,15},{3,1}... | collective-permute-start | bytes 1572872 | tf_op jit(solution)/shard_map/ppermute | solution.py:172
  43.1 15.1 %collective-permute-start.2 = (bf16[128,2048]{1,0:T(8,128)(2,1)S(1)}, bf16[128,2048]{1,0:T(8,128)(2,1)}, u32[]{:S(2)}, u32[]{:S(2)}) collective-permute-start(bf16[128,2048]{1,0:T(8,128)(2,1)S(1)} %collective-permute-done.1.refs_2_), channel_id=1, source_target_pairs={{0,1},{1,0},{2,3},{3,2},{4,5},{5,4},{6,7},{7,6},{8,9},{9,8},{10,11... | collective-permute-start | bytes 1572872 | tf_op jit(solution)/shard_map/ppermute | solution.py:174
  45.1 15.1 %collective-permute-start.6 = (bf16[128,2048]{1,0:T(8,128)(2,1)S(1)}, bf16[128,2048]{1,0:T(8,128)(2,1)}, u32[]{:S(2)}, u32[]{:S(2)}) collective-permute-start(bf16[128,2048]{1,0:T(8,128)(2,1)S(1)} %collective-permute-done.5.refs_6_), channel_id=1, source_target_pairs={{0,1},{1,0},{2,3},{3,2},{4,5},{5,4},{6,7},{7,6},{8,9},{9,8},{10,11... | collective-permute-start | bytes 1572872 | tf_op jit(solution)/shard_map/ppermute | solution.py:174
  47.5 15.1 %collective-permute-start.13 = (bf16[128,2048]{1,0:T(8,128)(2,1)}, bf16[128,2048]{1,0:T(8,128)(2,1)}, u32[]{:S(2)}, u32[]{:S(2)}) collective-permute-start(bf16[128,2048]{1,0:T(8,128)(2,1)} %collective-permute-done.9.refs_10_), channel_id=1, source_target_pairs={{0,2},{2,4},{4,6},{6,8},{8,10},{10,12},{12,14},{14,0},{1,15},{3,1}... | collective-permute-start | bytes 1572872 | tf_op jit(solution)/shard_map/ppermute | solution.py:172
  51.9 12.6 %collective-permute-start.11 = (bf16[128,2048]{1,0:T(8,128)(2,1)}, bf16[128,2048]{1,0:T(8,128)(2,1)}, u32[]{:S(2)}, u32[]{:S(2)}) collective-permute-start(bf16[128,2048]{1,0:T(8,128)(2,1)} %collective-permute-done.7.refs_8_), channel_id=1, source_target_pairs={{0,2},{2,4},{4,6},{6,8},{8,10},{10,12},{12,14},{14,0},{1,15},{3,1}... | collective-permute-start | bytes 1572872 | tf_op jit(solution)/shard_map/ppermute | solution.py:172
  54.5 0.7 copy-start.4
  55.2 13.1 %copy-start.3 = (s32[32]{0:T(128)S(1)}, s32[32]{0:T(128)}, u32[]{:S(2)}) copy-start(s32[32]{0:T(128)} %constant.94.clone) | copy-start | bytes 388
  55.2 13.9 %collective-permute-start.4 = (bf16[128,2048]{1,0:T(8,128)(2,1)}, bf16[128,2048]{1,0:T(8,128)(2,1)}, u32[]{:S(2)}, u32[]{:S(2)}) collective-permute-start(bf16[128,2048]{1,0:T(8,128)(2,1)} %copy-done.1), channel_id=1, source_target_pairs={{0,1},{1,0},{2,3},{3,2},{4,5},{5,4},{6,7},{7,6},{8,9},{9,8},{10,11... | collective-permute-start | bytes 1572872 | tf_op jit(solution)/shard_map/ppermute | solution.py:174
  58.2 10.9 %collective-permute-start.10 = (bf16[128,2048]{1,0:T(8,128)(2,1)}, bf16[128,2048]{1,0:T(8,128)(2,1)}, u32[]{:S(2)}, u32[]{:S(2)}) collective-permute-start(bf16[128,2048]{1,0:T(8,128)(2,1)} %collective-permute-done.9.refs_10_), channel_id=1, source_target_pairs={{0,1},{1,0},{2,3},{3,2},{4,5},{5,4},{6,7},{7,6},{8,9},{9,8},{10,11... | collective-permute-start | bytes 1572872 | tf_op jit(solution)/shard_map/ppermute | solution.py:174
  60.2 9.0 %collective-permute-start.8 = (bf16[128,2048]{1,0:T(8,128)(2,1)}, bf16[128,2048]{1,0:T(8,128)(2,1)}, u32[]{:S(2)}, u32[]{:S(2)}) collective-permute-start(bf16[128,2048]{1,0:T(8,128)(2,1)} %collective-permute-done.7.refs_8_), channel_id=1, source_target_pairs={{0,1},{1,0},{2,3},{3,2},{4,5},{5,4},{6,7},{7,6},{8,9},{9,8},{10,11... | collective-permute-start | bytes 1572872 | tf_op jit(solution)/shard_map/ppermute | solution.py:174
  62.6 6.6 %collective-permute-start.14 = (bf16[128,2048]{1,0:T(8,128)(2,1)}, bf16[128,2048]{1,0:T(8,128)(2,1)}, u32[]{:S(2)}, u32[]{:S(2)}) collective-permute-start(bf16[128,2048]{1,0:T(8,128)(2,1)} %collective-permute-done.13.refs_14_), channel_id=1, source_target_pairs={{0,1},{1,0},{2,3},{3,2},{4,5},{5,4},{6,7},{7,6},{8,9},{9,8},{10,11... | collective-permute-start | bytes 1572872 | tf_op jit(solution)/shard_map/ppermute | solution.py:174
  64.5 5.5 %collective-permute-start.12 = (bf16[128,2048]{1,0:T(8,128)(2,1)}, bf16[128,2048]{1,0:T(8,128)(2,1)}, u32[]{:S(2)}, u32[]{:S(2)}) collective-permute-start(bf16[128,2048]{1,0:T(8,128)(2,1)} %collective-permute-done.11.refs_12_), channel_id=1, source_target_pairs={{0,1},{1,0},{2,3},{3,2},{4,5},{5,4},{6,7},{7,6},{8,9},{9,8},{10,11... | collective-permute-start | bytes 1572872 | tf_op jit(solution)/shard_map/ppermute | solution.py:174
  70.0 1.0 %copy-start.2 = (bf16[128,2048]{1,0:T(8,128)(2,1)S(1)}, bf16[128,2048]{1,0:T(8,128)(2,1)}, u32[]{:S(2)}) copy-start(bf16[128,2048]{1,0:T(8,128)(2,1)} %copy-done.1) | copy-start | bytes 1572868

commit v2 on v1

v2 whole, which is shorter than its diff:
```python
import math

import jax
import jax.numpy as jnp
import numpy as np
from jax import lax
from jax.experimental import pallas as pl
from jax.experimental.pallas import tpu as pltpu
from jax.sharding import PartitionSpec as P

HEADS = 32
KVH = 4
GROUP = HEADS // KVH
DH = 128
BLK = 128
WIDTH = KVH * DH
SEQ = 16
CHIPS = SEQ // 2
SCALE = math.log2(math.e) / math.sqrt(DH)

RING = [(2 * z, 2 * ((z + 1) % CHIPS)) for z in range(CHIPS)] + [
    (2 * z + 1, 2 * ((z - 1) % CHIPS) + 1) for z in range(CHIPS)
]
CROSS = [(2 * z + 1, 2 * ((z + 1) % CHIPS)) for z in range(CHIPS)] + [
    (2 * z, 2 * ((z - 1) % CHIPS) + 1) for z in range(CHIPS)
]
SWAP = [(i, i ^ 1) for i in range(SEQ)]

NAMES = ["own", "oth"] + [
    kind + str(step) + lane
    for step in (1, 2, 3, 4)
    for lane in ("A", "B")
    for kind in ("got", "swp")
    if (step, lane) != (4, "B")
]


def slot_table():
    table = np.zeros((2, CHIPS, 2), np.int32)
    for core in range(2):
        for away in range(CHIPS):
            for owner in range(2):
                if away == 0:
                    name = "own" if owner == core else "oth"
                else:
                    down = away < 4 or (away == 4 and owner == 1)
                    step = away if down else CHIPS - away
                    lane = "A" if owner == (1 if down else 0) else "B"
                    kind = "got" if core == (1 if down else 0) else "swp"
                    name = kind + str(step) + lane
                table[core, away, owner] = NAMES.index(name)
    return table


def pick(slot, low, high, use):
    if high - low == 1:
        use(low)
        return
    middle = (low + high) // 2

    @pl.when(slot < middle)
    def _():
        pick(slot, low, middle, use)

    @pl.when(slot >= middle)
    def _():
        pick(slot, middle, high, use)


def join_kernel(*refs):
    parts, joined, sems = refs[:4], refs[4], refs[5]
    copies = [
        pltpu.make_async_copy(part, joined.at[:, n * WIDTH : (n + 1) * WIDTH], sems.at[n])
        for n, part in enumerate(parts)
    ]
    for copy in copies:
        copy.start()
    for copy in copies:
        copy.wait()


def join(parts):
    return pl.pallas_call(
        join_kernel,
        out_shape=jax.ShapeDtypeStruct((BLK, 4 * WIDTH), jnp.bfloat16),
        in_specs=[pl.BlockSpec(memory_space=pltpu.HBM)] * 4,
        out_specs=pl.BlockSpec(memory_space=pltpu.VMEM),
        scratch_shapes=[pltpu.SemaphoreType.DMA((4,))],
        compiler_params=pltpu.CompilerParams(vmem_limit_bytes=60 << 20),
        cost_estimate=pl.CostEstimate(flops=0, bytes_accessed=1 << 20, transcendentals=0),
    )(*parts)


OVER_ROWS = (((1,), (1,)), ((), ()))
OVER_KEYS = (((1,), (0,)), ((), ()))


def head_columns(h):
    return slice(h * DH, (h + 1) * DH)


def group_queries(q_ref, g):
    return jnp.concatenate([q_ref[:, head_columns(h)] for h in range(g * GROUP, (g + 1) * GROUP)], axis=0)


def near_kernel(
    me_ref, table_ref, lists_ref, q_ref, own_ref, oth_ref, got_ref, total_ref, sum_ref, top_ref, slot_ref, half_ref, new, old, sems
):
    me = me_ref[0]
    core = lax.rem(me, 2)
    column = pl.multiple_of(jnp.where(me == 0, 0, 2 * WIDTH), 2 * WIDTH)
    own_copy = pltpu.make_async_copy(own_ref.at[:, 2 * WIDTH :], new, sems.at[0])
    own_copy.start()

    def old_copy(source):
        return pltpu.make_async_copy(source.at[:, pl.ds(column, 2 * WIDTH)], old, sems.at[1])

    @pl.when(core == 1)
    def _():
        old_copy(oth_ref).start()

    @pl.when(core == 0)
    def _():
        old_copy(got_ref).start()

    def locate(h, carry):
        chosen = lists_ref[4 * h] + lists_ref[4 * h + 1] + lists_ref[4 * h + 2] + lists_ref[4 * h + 3]
        chosen = jnp.clip(chosen - (2 * (SEQ + me) - 1), 0, 2 * SEQ - 1)
        owner = lax.rem(chosen, SEQ)
        away = lax.rem(owner // 2 - me // 2 + CHIPS, CHIPS)
        slot_ref[h] = table_ref[core * 2 * CHIPS + away * 2 + lax.rem(owner, 2)]
        half_ref[h] = chosen // SEQ
        return carry

    lax.fori_loop(0, HEADS, locate, 0)
    own_copy.wait()
    old_copy(oth_ref).wait()

    seen = lax.broadcasted_iota(jnp.int32, (BLK, BLK), 1) <= lax.broadcasted_iota(jnp.int32, (BLK, BLK), 0)
    ones = jnp.ones((2 * BLK, DH), jnp.bfloat16)
    for h in range(HEADS):
        g, cols = h // GROUP, head_columns(h)
        keys = jnp.concatenate([old[:, head_columns(g)], new[:, head_columns(g)]], axis=0)
        values = jnp.concatenate([old[:, head_columns(KVH + g)], new[:, head_columns(KVH + g)]], axis=0)
        scores = lax.dot_general(q_ref[:, cols], keys, OVER_ROWS, preferred_element_type=jnp.float32)
        scores = jnp.concatenate([scores[:, :BLK], jnp.where(seen, scores[:, BLK:], -jnp.inf)], axis=1)
        top = jnp.max(scores, axis=1, keepdims=True)
        powers = jnp.exp2((scores - top) * SCALE).astype(jnp.bfloat16)
        mixed = lax.dot_general(
            powers, jnp.concatenate([values, ones], axis=1), OVER_KEYS, preferred_element_type=jnp.float32
        )
        total_ref[:, cols] = mixed[:, :DH]
        sum_ref[:, cols] = mixed[:, DH:]
        top_ref[:, cols] = jnp.broadcast_to(top, (BLK, DH))


def near(me, table, lists, queries, own, oth, got):
    smem, vmem = pl.BlockSpec(memory_space=pltpu.SMEM), pl.BlockSpec(memory_space=pltpu.VMEM)
    anywhere = pl.BlockSpec(memory_space=pl.ANY)
    return pl.pallas_call(
        near_kernel,
        out_shape=[
            jax.ShapeDtypeStruct((BLK, HEADS * DH), jnp.float32),
            jax.ShapeDtypeStruct((BLK, HEADS * DH), jnp.float32),
            jax.ShapeDtypeStruct((BLK, HEADS * DH), jnp.float32),
            jax.ShapeDtypeStruct((HEADS,), jnp.int32),
            jax.ShapeDtypeStruct((HEADS,), jnp.int32),
        ],
        in_specs=[smem] * 3 + [vmem] + [anywhere] * 3,
        out_specs=[vmem, vmem, vmem, smem, smem],
        scratch_shapes=[
            pltpu.VMEM((BLK, 2 * WIDTH), jnp.bfloat16),
            pltpu.VMEM((BLK, 2 * WIDTH), jnp.bfloat16),
            pltpu.SemaphoreType.DMA((2,)),
        ],
        compiler_params=pltpu.CompilerParams(vmem_limit_bytes=20 << 20),
        cost_estimate=pl.CostEstimate(flops=1 << 29, bytes_accessed=4 << 20, transcendentals=1 << 20),
    )(me, table, lists, queries, own, oth, got)


def far_kernel(me_ref, table_ref, slot_ref, half_ref, q_ref, total_ref, sum_ref, top_ref, *refs):
    held = refs[: len(NAMES)]
    o_ref, first, k_pick, v_pick = refs[len(NAMES) :]
    me = me_ref[0]
    slot = table_ref[lax.rem(me, 2) * 2 * CHIPS + lax.rem(CHIPS - me // 2, CHIPS) * 2]

    def take_first(b):
        first[...] = held[b][:, : 2 * WIDTH]

    pick(slot, 0, len(NAMES), take_first)

    def take_head(h, carry):
        column = pl.multiple_of(half_ref[h] * 2 * WIDTH + (h // GROUP) * DH, DH)

        def take(b):
            k_pick[h] = held[b][:, pl.ds(column, DH)]
            v_pick[h] = held[b][:, pl.ds(column + WIDTH, DH)]

        pick(slot_ref[h], 0, len(NAMES), take)
        return carry

    lax.fori_loop(0, HEADS, take_head, 0, unroll=4)
    ones = jnp.ones((2 * BLK, DH), jnp.bfloat16)
    for h in range(HEADS):
        g, cols = h // GROUP, head_columns(h)
        keys = jnp.concatenate([first[:, head_columns(g)], k_pick[h]], axis=0)
        values = jnp.concatenate([first[:, head_columns(KVH + g)], v_pick[h]], axis=0)
        scores = lax.dot_general(q_ref[:, cols], keys, OVER_ROWS, preferred_element_type=jnp.float32)
        top = jnp.maximum(jnp.max(scores, axis=1, keepdims=True), top_ref[:, cols])
        powers = jnp.exp2((scores - jnp.concatenate([top, top], axis=1)) * SCALE).astype(jnp.bfloat16)
        factor = jnp.exp2((top_ref[:, cols] - top) * SCALE)
        mixed = lax.dot_general(
            powers, jnp.concatenate([values, ones], axis=1), OVER_KEYS, preferred_element_type=jnp.float32
        )
        total = mixed[:, :DH] + factor * total_ref[:, cols]
        weight = mixed[:, DH:] + factor * sum_ref[:, cols]
        o_ref[:, cols] = (total / weight).astype(jnp.bfloat16)


def tie_kernel(through_in, after, through_out):
    pass


def tie(through, after):
    return pl.pallas_call(
        tie_kernel,
        out_shape=jax.ShapeDtypeStruct(through.shape, through.dtype),
        in_specs=[pl.BlockSpec(memory_space=pl.ANY)] * 2,
        out_specs=pl.BlockSpec(memory_space=pl.ANY),
        input_output_aliases={0: 0},
        compiler_params=pltpu.CompilerParams(vmem_limit_bytes=1 << 20),
    )(through, after)


def far(me, table, slots, halves, queries, near_parts, held):
    smem, vmem = pl.BlockSpec(memory_space=pltpu.SMEM), pl.BlockSpec(memory_space=pltpu.VMEM)
    return pl.pallas_call(
        far_kernel,
        out_shape=jax.ShapeDtypeStruct((BLK, HEADS * DH), jnp.bfloat16),
        in_specs=[smem] * 4 + [vmem] * (4 + len(NAMES)),
        out_specs=vmem,
        scratch_shapes=[
            pltpu.VMEM((BLK, 2 * WIDTH), jnp.bfloat16),
            pltpu.VMEM((HEADS, BLK, DH), jnp.bfloat16),
            pltpu.VMEM((HEADS, BLK, DH), jnp.bfloat16),
        ],
        compiler_params=pltpu.CompilerParams(vmem_limit_bytes=24 << 20),
        cost_estimate=pl.CostEstimate(flops=1 << 29, bytes_accessed=6 << 20, transcendentals=1 << 20),
    )(me, table, slots, halves, queries, *near_parts, *held)


def shards(queries, span_keys, span_values, cache_keys, cache_values, block_lists):
    me = lax.axis_index("seq").astype(jnp.int32).reshape(1)
    table = jnp.asarray(slot_table().reshape(-1))
    own = join([cache_keys, cache_values, span_keys, span_values])
    held = {"own": own}
    last = {}
    for step in (1, 2, 3, 4):
        for lane in ("A", "B"):
            if (step, lane) == (4, "B"):
                continue
            if step == 1:
                last[lane] = lax.ppermute(own, "seq", RING if lane == "A" else CROSS)
            else:
                if (step, lane) == (3, "A"):
                    last[lane] = tie(last[lane], slots)
                    held["got2A"] = last[lane]
                    held["swp2A"] = lax.ppermute(last[lane], "seq", SWAP)
                last[lane] = lax.ppermute(last[lane], "seq", RING)
            held["got" + str(step) + lane] = last[lane]
            if (step, lane) == (1, "B"):
                held["oth"] = lax.ppermute(own, "seq", SWAP)
                total, sums, tops, slots, halves = near(
                    me, table, block_lists.reshape(-1), queries, own, held["oth"], held["got1B"]
                )
            if (step, lane) != (2, "A"):
                held["swp" + str(step) + lane] = lax.ppermute(last[lane], "seq", SWAP)
    return far(me, table, slots, halves, queries, (total, sums, tops), [held[name] for name in NAMES])


def solution(mesh):
    rows = P(("req", "seq"), None)
    return jax.shard_map(
        shards,
        mesh=mesh,
        in_specs=(rows,) * 5 + (P(("req", "seq"), None, None),),
        out_specs=rows,
        check_vma=False,
    )
```

time: 80.4 us -> 72.1 us (0.90)
  waiting for transfers between devices: 9.77 us -> 6.21 us
  starting transfers between devices: 54.5 us -> 51.1 us
  local copies, waits for them, and re-layouts: 6.26 us -> 3.79 us
  Pallas kernels: 8.75 us -> 10.1 us
    ppermute x7 -> x5, starting transfers between devices: 35.4 us -> 16.1 us  [shards(): last[lane] = lax.ppermute(last[lane], 'seq', RING)]
    ppermute x1 -> x4, starting transfers between devices: 1.92 us -> 19.4 us  [the longest x2 13.4 us: shards(): last[lane] = lax.ppermute(own, 'seq', RING if lane == 'A' else CROSS)]
    ppermute x7 -> x5, waiting for transfers between devices: 8.95 us -> 0.01 us  [shards(): last[lane] = lax.ppermute(last[lane], 'seq', RING)]
    ppermute x1 -> x4, waiting for transfers between devices: 0.01 us -> 4.72 us  [the longest x2 4.71 us: shards(): last[lane] = lax.ppermute(own, 'seq', RING if lane == 'A' else CROSS)]
    ppermute x7 -> x6, starting transfers between devices: 17.2 us -> 15.6 us  [shards(): held['swp' + str(step) + lane] = lax.ppermute(last[lane], 'seq', SWAP)]
    pallas_call x1 -> x4, Pallas kernels: 8.75 us -> 10.1 us  [the longest x1 5.1 us: far(): pl.pallas_call(far_kernel, out_shape=jax.ShapeDtypeStruct((BLK, HEADS * D...]
    concatenate x1 -> x0, local copies, waits for them, and re-layouts: 0.92 us -> none  [shards(): jnp.concatenate([cache_keys, cache_values, span_keys, span_values], axis=1)]
    unnamed x13 -> x11, local copies, waits for them, and re-layouts: 4.56 us -> 3.69 us
  transfers between devices with their start and end apart: 15 -> 15, of which waited for: 4 -> 2; matrix products, arithmetic and copies ran while one was open for 1% -> 1% of each run, Pallas kernels for 0% -> 4%
where the time goes in v2:
time: 72.1 us; the launch traced here: 71.4 us
  starting transfers between devices  51.1 us (71%)
  Pallas kernels  10.1 us (14%)
  waiting for transfers between devices  6.21 us (9%)
  local copies, waits for them, and re-layouts  3.79 us (5%)
    ppermute x5, starting transfers between devices, shards(): last[lane] = lax.ppermute(last[lane], 'seq', RING)  16.1 us
    ppermute x6, starting transfers between devices, shards(): held['swp' + str(step) + lane] = lax.ppermute(last[lane], 'seq', SWAP)  15.6 us
    ppermute x2, starting transfers between devices, shards(): last[lane] = lax.ppermute(own, 'seq', RING if lane == 'A' else CROSS)  13.4 us
    pallas_call x1, Pallas kernels, far(): pl.pallas_call(far_kernel, out_shape=jax.ShapeDtypeStruct((BLK, HEADS * D...  5.1 us
    ppermute x2, waiting for transfers between devices, shards(): last[lane] = lax.ppermute(own, 'seq', RING if lane == 'A' else CROSS)  4.71 us
    unnamed x11, local copies, waits for them, and re-layouts  3.69 us
    ppermute x1, starting transfers between devices, shards(): held['swp2A'] = lax.ppermute(last[lane], 'seq', SWAP)  3.41 us
    pallas_call x1, Pallas kernels, near(): pl.pallas_call(near_kernel, out_shape=[jax.ShapeDtypeStruct((BLK, HEADS *...  2.96 us
  transfers between devices with their start and end apart: 15, of which 2 were waited for; matrix products, arithmetic and copies ran while one was open for 1% of the time, Pallas kernels for 4%

profile of v2, /device:TPU:1, one launch (start us, length us, event | category | flops | bytes accessed | tf_op | source)
XLA Modules:
  0.0 71.4 jit_solution(16863609875213999515)
XLA Ops:
  0.0 2.0 %shard_map.73.own_ref.refs_0_ = bf16[128,2048]{1,0:T(8,128)(2,1)} custom-call(bf16[128,512]{1,0:T(8,128)(2,1)} %refs_0_.1, bf16[128,512]{1,0:T(8,128)(2,1)} %refs_1_.1, bf16[128,512]{1,0:T(8,128)(2,1)} %refs_2_.1, bf16[128,512]{1,0:T(8,128)(2,1)} %refs_3_.1), custom_call_target="tpu_custom_call" | custom-call | bytes 1048576 | tf_op jit(solution)/shard_map/pallas_call | solution.py:83
  2.0 11.5 %collective-permute-start.2 = (bf16[128,2048]{1,0:T(8,128)(2,1)}, bf16[128,2048]{1,0:T(8,128)(2,1)S(1)}, u32[]{:S(2)}, u32[]{:S(2)}) collective-permute-start(bf16[128,2048]{1,0:T(8,128)(2,1)} %shard_map.73.own_ref.refs_0_), channel_id=1, source_target_pairs={{0,2},{2,4},{4,6},{6,8},{8,10},{10,12},{12,14},{14,0},{1,15},{3,1}... | collective-permute-start | bytes 1572872 | tf_op jit(solution)/shard_map/ppermute | solution.py:263
  13.5 1.9 %collective-permute-start.1 = (bf16[128,2048]{1,0:T(8,128)(2,1)}, bf16[128,2048]{1,0:T(8,128)(2,1)S(1)}, u32[]{:S(2)}, u32[]{:S(2)}) collective-permute-start(bf16[128,2048]{1,0:T(8,128)(2,1)} %shard_map.73.own_ref.refs_0_), channel_id=1, source_target_pairs={{1,2},{3,4},{5,6},{7,8},{9,10},{11,12},{13,14},{15,0},{0,15},{2,1}... | collective-permute-start | bytes 1572872 | tf_op jit(solution)/shard_map/ppermute | solution.py:263
  15.5 2.6 %collective-permute-start = (bf16[128,2048]{1,0:T(8,128)(2,1)}, bf16[128,2048]{1,0:T(8,128)(2,1)S(1)}, u32[]{:S(2)}, u32[]{:S(2)}) collective-permute-start(bf16[128,2048]{1,0:T(8,128)(2,1)} %shard_map.73.own_ref.refs_0_), channel_id=1, source_target_pairs={{0,1},{1,0},{2,3},{3,2},{4,5},{5,4},{6,7},{7,6},{8,9},{9,8},{10,11... | collective-permute-start | bytes 1572872 | tf_op jit(solution)/shard_map/ppermute | solution.py:272
  18.0 4.7 %collective-permute-done.2.refs_2_ = bf16[128,2048]{1,0:T(8,128)(2,1)S(1)} collective-permute-done((bf16[128,2048]{1,0:T(8,128)(2,1)}, bf16[128,2048]{1,0:T(8,128)(2,1)S(1)}, u32[]{:S(2)}, u32[]{:S(2)}) %collective-permute-start.2) | collective-permute-done | bytes 524320 | tf_op jit(solution)/shard_map/ppermute | solution.py:263
  22.7 4.9 %collective-permute-start.5 = (bf16[128,2048]{1,0:T(8,128)(2,1)S(1)}, bf16[128,2048]{1,0:T(8,128)(2,1)S(1)}, u32[]{:S(2)}, u32[]{:S(2)}) collective-permute-start(bf16[128,2048]{1,0:T(8,128)(2,1)S(1)} %collective-permute-done.2.refs_2_), channel_id=1, source_target_pairs={{0,2},{2,4},{4,6},{6,8},{8,10},{10,12},{12,14},{14,0},{1,15},{3,1}... | collective-permute-start | bytes 1572872 | tf_op jit(solution)/shard_map/ppermute | solution.py:269
  27.6 0.8 %copy.10 = s32[1,32,4]{2,1,0:T(8,128)S(1)} copy(s32[1,32,4]{1,2,0:T(4,128)} %param.12) | data formatting | bytes 1024 | tf_op args[5]
  28.5 1.9 %collective-permute-start.7 = (bf16[128,2048]{1,0:T(8,128)(2,1)S(1)}, bf16[128,2048]{1,0:T(8,128)(2,1)S(1)}, u32[]{:S(2)}, u32[]{:S(2)}) collective-permute-start(bf16[128,2048]{1,0:T(8,128)(2,1)S(1)} %collective-permute-done.1.got_ref.refs_4_), channel_id=1, source_target_pairs={{0,2},{2,4},{4,6},{6,8},{8,10},{10,12},{12,14},{14,0},{1,15},{3,1}... | collective-permute-start | bytes 1572872 | tf_op jit(solution)/shard_map/ppermute | solution.py:269
  30.5 1.0 %copy-done = bf16[128,2048]{1,0:T(8,128)(2,1)S(1)} copy-done((bf16[128,2048]{1,0:T(8,128)(2,1)S(1)}, bf16[128,2048]{1,0:T(8,128)(2,1)}, u32[]{:S(2)}) %copy-start) | copy-done | bytes 524312
  31.5 1.2 %copy-done.2 = bf16[128,4096]{1,0:T(8,128)(2,1)S(1)} copy-done((bf16[128,4096]{1,0:T(8,128)(2,1)S(1)}, bf16[128,4096]{1,0:T(8,128)(2,1)}, u32[]{:S(2)}) %copy-start.2) | copy-done | bytes 1048600
  32.8 0.7 copy-done.4
  33.4 3.0 %shard_map.74 = (f32[128,4096]{1,0:T(8,128)S(1)}, f32[128,4096]{1,0:T(8,128)S(1)}, f32[128,4096]{1,0:T(8,128)S(1)}, s32[32]{0:T(128)S(1)}, s32[32]{0:T(128)S(1)}) custom-call(s32[1]{0:T(128)} %bitcast.me_ref, s32[32]{0:T(128)S(1)} %copy-done.4, s32[128]{0:T(128)S(1)} %reshape.7.lists_ref, bf16[128,4096]{1,0:T(8,128)(2,1)S(1)} %copy-done.2, ...), custom_call_target="tpu_custom_call" | custom-call | flops 536870912 | bytes 4194304 | tf_op jit(solution)/shard_map/pallas_call | solution.py:160
  36.4 2.4 %collective-permute-start.9 = (bf16[128,2048]{1,0:T(8,128)(2,1)S(1)}, bf16[128,2048]{1,0:T(8,128)(2,1)S(1)}, u32[]{:S(2)}, u32[]{:S(2)}) collective-permute-start(bf16[128,2048]{1,0:T(8,128)(2,1)S(1)} %shard_map.75.refs_6_), channel_id=1, source_target_pairs={{0,2},{2,4},{4,6},{6,8},{8,10},{10,12},{12,14},{14,0},{1,15},{3,1}... | collective-permute-start | bytes 1572872 | tf_op jit(solution)/shard_map/ppermute | solution.py:269
  38.8 3.4 %collective-permute-start.3 = (bf16[128,2048]{1,0:T(8,128)(2,1)S(1)}, bf16[128,2048]{1,0:T(8,128)(2,1)S(1)}, u32[]{:S(2)}, u32[]{:S(2)}) collective-permute-start(bf16[128,2048]{1,0:T(8,128)(2,1)S(1)} %collective-permute-done.2.refs_2_), channel_id=1, source_target_pairs={{0,1},{1,0},{2,3},{3,2},{4,5},{5,4},{6,7},{7,6},{8,9},{9,8},{10,11... | collective-permute-start | bytes 1572872 | tf_op jit(solution)/shard_map/ppermute | solution.py:277
  42.2 1.9 %collective-permute-start.4 = (bf16[128,2048]{1,0:T(8,128)(2,1)S(1)}, bf16[128,2048]{1,0:T(8,128)(2,1)S(1)}, u32[]{:S(2)}, u32[]{:S(2)}) collective-permute-start(bf16[128,2048]{1,0:T(8,128)(2,1)S(1)} %collective-permute-done.1.got_ref.refs_4_), channel_id=1, source_target_pairs={{0,1},{1,0},{2,3},{3,2},{4,5},{5,4},{6,7},{7,6},{8,9},{9,8},{10,11... | collective-permute-start | bytes 1572872 | tf_op jit(solution)/shard_map/ppermute | solution.py:277
  44.1 4.9 %collective-permute-start.11 = (bf16[128,2048]{1,0:T(8,128)(2,1)S(1)}, bf16[128,2048]{1,0:T(8,128)(2,1)S(1)}, u32[]{:S(2)}, u32[]{:S(2)}) collective-permute-start(bf16[128,2048]{1,0:T(8,128)(2,1)S(1)} %collective-permute-done.7.refs_8_), channel_id=1, source_target_pairs={{0,2},{2,4},{4,6},{6,8},{8,10},{10,12},{12,14},{14,0},{1,15},{3,1}... | collective-permute-start | bytes 1572872 | tf_op jit(solution)/shard_map/ppermute | solution.py:269
  49.0 2.0 %collective-permute-start.13 = (bf16[128,2048]{1,0:T(8,128)(2,1)S(1)}, bf16[128,2048]{1,0:T(8,128)(2,1)S(1)}, u32[]{:S(2)}, u32[]{:S(2)}) collective-permute-start(bf16[128,2048]{1,0:T(8,128)(2,1)S(1)} %collective-permute-done.9.refs_10_), channel_id=1, source_target_pairs={{0,2},{2,4},{4,6},{6,8},{8,10},{10,12},{12,14},{14,0},{1,15},{3,1}... | collective-permute-start | bytes 1572872 | tf_op jit(solution)/shard_map/ppermute | solution.py:269
  51.0 3.4 %collective-permute-start.6 = (bf16[128,2048]{1,0:T(8,128)(2,1)S(1)}, bf16[128,2048]{1,0:T(8,128)(2,1)S(1)}, u32[]{:S(2)}, u32[]{:S(2)}) collective-permute-start(bf16[128,2048]{1,0:T(8,128)(2,1)S(1)} %shard_map.75.refs_6_), channel_id=1, source_target_pairs={{0,1},{1,0},{2,3},{3,2},{4,5},{5,4},{6,7},{7,6},{8,9},{9,8},{10,11... | collective-permute-start | bytes 1572872 | tf_op jit(solution)/shard_map/ppermute | solution.py:268
  54.5 1.9 %collective-permute-start.8 = (bf16[128,2048]{1,0:T(8,128)(2,1)S(1)}, bf16[128,2048]{1,0:T(8,128)(2,1)S(1)}, u32[]{:S(2)}, u32[]{:S(2)}) collective-permute-start(bf16[128,2048]{1,0:T(8,128)(2,1)S(1)} %collective-permute-done.7.refs_8_), channel_id=1, source_target_pairs={{0,1},{1,0},{2,3},{3,2},{4,5},{5,4},{6,7},{7,6},{8,9},{9,8},{10,11... | collective-permute-start | bytes 1572872 | tf_op jit(solution)/shard_map/ppermute | solution.py:277
  56.4 2.4 %collective-permute-start.10 = (bf16[128,2048]{1,0:T(8,128)(2,1)S(1)}, bf16[128,2048]{1,0:T(8,128)(2,1)S(1)}, u32[]{:S(2)}, u32[]{:S(2)}) collective-permute-start(bf16[128,2048]{1,0:T(8,128)(2,1)S(1)} %collective-permute-done.9.refs_10_), channel_id=1, source_target_pairs={{0,1},{1,0},{2,3},{3,2},{4,5},{5,4},{6,7},{7,6},{8,9},{9,8},{10,11... | collective-permute-start | bytes 1572872 | tf_op jit(solution)/shard_map/ppermute | solution.py:277
  58.8 1.9 %collective-permute-start.12 = (bf16[128,2048]{1,0:T(8,128)(2,1)S(1)}, bf16[128,2048]{1,0:T(8,128)(2,1)S(1)}, u32[]{:S(2)}, u32[]{:S(2)}) collective-permute-start(bf16[128,2048]{1,0:T(8,128)(2,1)S(1)} %collective-permute-done.11.refs_12_), channel_id=1, source_target_pairs={{0,1},{1,0},{2,3},{3,2},{4,5},{5,4},{6,7},{7,6},{8,9},{9,8},{10,11... | collective-permute-start | bytes 1572872 | tf_op jit(solution)/shard_map/ppermute | solution.py:277
  60.8 4.0 %collective-permute-start.14 = (bf16[128,2048]{1,0:T(8,128)(2,1)S(1)}, bf16[128,2048]{1,0:T(8,128)(2,1)S(1)}, u32[]{:S(2)}, u32[]{:S(2)}) collective-permute-start(bf16[128,2048]{1,0:T(8,128)(2,1)S(1)} %collective-permute-done.13.refs_14_), channel_id=1, source_target_pairs={{0,1},{1,0},{2,3},{3,2},{4,5},{5,4},{6,7},{7,6},{8,9},{9,8},{10,11... | collective-permute-start | bytes 1572872 | tf_op jit(solution)/shard_map/ppermute | solution.py:277
  64.8 1.5 %collective-permute-done.14.refs_15_ = bf16[128,2048]{1,0:T(8,128)(2,1)S(1)} collective-permute-done((bf16[128,2048]{1,0:T(8,128)(2,1)S(1)}, bf16[128,2048]{1,0:T(8,128)(2,1)S(1)}, u32[]{:S(2)}, u32[]{:S(2)}) %collective-permute-start.14) | collective-permute-done | bytes 524320 | tf_op jit(solution)/shard_map/ppermute | solution.py:277
  66.3 5.1 %shard_map.76 = bf16[128,4096]{1,0:T(8,128)(2,1)} custom-call(s32[1]{0:T(128)} %bitcast.me_ref, s32[32]{0:T(128)S(1)} %copy-done.4, s32[32]{0:T(128)S(1)} %get-tuple-element.10.after.slot_ref, s32[32]{0:T(128)S(1)} %get-tuple-element.11.half_ref, bf16[128,4096]{1,0:T(8,128)(2,1)S(1)} %copy-done.3, f32[128,4096]{1,0:T(8,128)S(1)} %get-tuple-element.12.total_ref, ...), custom_call_target="tpu_custom_call" | custom-call | flops 536870912 | bytes 6291456 | tf_op jit(solution)/shard_map/pallas_call | solution.py:237
  (22 shorter events, 0.2 us)
Async XLA Ops:
  0.0 66.3 %copy-start.3 = (bf16[128,4096]{1,0:T(8,128)(2,1)S(1)}, bf16[128,4096]{1,0:T(8,128)(2,1)}, u32[]{:S(2)}) copy-start(bf16[128,4096]{1,0:T(8,128)(2,1)} %q_ref.3) | copy-start | bytes 3145732
  2.0 20.7 %collective-permute-start.2 = (bf16[128,2048]{1,0:T(8,128)(2,1)}, bf16[128,2048]{1,0:T(8,128)(2,1)S(1)}, u32[]{:S(2)}, u32[]{:S(2)}) collective-permute-start(bf16[128,2048]{1,0:T(8,128)(2,1)} %shard_map.73.own_ref.refs_0_), channel_id=1, source_target_pairs={{0,2},{2,4},{4,6},{6,8},{8,10},{10,12},{12,14},{14,0},{1,15},{3,1}... | collective-permute-start | bytes 1572872 | tf_op jit(solution)/shard_map/ppermute | solution.py:263
  13.5 15.0 %collective-permute-start.1 = (bf16[128,2048]{1,0:T(8,128)(2,1)}, bf16[128,2048]{1,0:T(8,128)(2,1)S(1)}, u32[]{:S(2)}, u32[]{:S(2)}) collective-permute-start(bf16[128,2048]{1,0:T(8,128)(2,1)} %shard_map.73.own_ref.refs_0_), channel_id=1, source_target_pairs={{1,2},{3,4},{5,6},{7,8},{9,10},{11,12},{13,14},{15,0},{0,15},{2,1}... | collective-permute-start | bytes 1572872 | tf_op jit(solution)/shard_map/ppermute | solution.py:263
  15.5 15.0 %collective-permute-start = (bf16[128,2048]{1,0:T(8,128)(2,1)}, bf16[128,2048]{1,0:T(8,128)(2,1)S(1)}, u32[]{:S(2)}, u32[]{:S(2)}) collective-permute-start(bf16[128,2048]{1,0:T(8,128)(2,1)} %shard_map.73.own_ref.refs_0_), channel_id=1, source_target_pairs={{0,1},{1,0},{2,3},{3,2},{4,5},{5,4},{6,7},{7,6},{8,9},{9,8},{10,11... | collective-permute-start | bytes 1572872 | tf_op jit(solution)/shard_map/ppermute | solution.py:272
  22.7 13.7 %collective-permute-start.5 = (bf16[128,2048]{1,0:T(8,128)(2,1)S(1)}, bf16[128,2048]{1,0:T(8,128)(2,1)S(1)}, u32[]{:S(2)}, u32[]{:S(2)}) collective-permute-start(bf16[128,2048]{1,0:T(8,128)(2,1)S(1)} %collective-permute-done.2.refs_2_), channel_id=1, source_target_pairs={{0,2},{2,4},{4,6},{6,8},{8,10},{10,12},{12,14},{14,0},{1,15},{3,1}... | collective-permute-start | bytes 1572872 | tf_op jit(solution)/shard_map/ppermute | solution.py:269
  28.5 15.6 %collective-permute-start.7 = (bf16[128,2048]{1,0:T(8,128)(2,1)S(1)}, bf16[128,2048]{1,0:T(8,128)(2,1)S(1)}, u32[]{:S(2)}, u32[]{:S(2)}) collective-permute-start(bf16[128,2048]{1,0:T(8,128)(2,1)S(1)} %collective-permute-done.1.got_ref.refs_4_), channel_id=1, source_target_pairs={{0,2},{2,4},{4,6},{6,8},{8,10},{10,12},{12,14},{14,0},{1,15},{3,1}... | collective-permute-start | bytes 1572872 | tf_op jit(solution)/shard_map/ppermute | solution.py:269
  30.5 1.0 %copy-start = (bf16[128,2048]{1,0:T(8,128)(2,1)S(1)}, bf16[128,2048]{1,0:T(8,128)(2,1)}, u32[]{:S(2)}) copy-start(bf16[128,2048]{1,0:T(8,128)(2,1)} %shard_map.73.own_ref.refs_0_) | copy-start | bytes 1572868
  31.5 1.2 %copy-start.2 = (bf16[128,4096]{1,0:T(8,128)(2,1)S(1)}, bf16[128,4096]{1,0:T(8,128)(2,1)}, u32[]{:S(2)}) copy-start(bf16[128,4096]{1,0:T(8,128)(2,1)} %q_ref.3) | copy-start | bytes 3145732
  32.8 0.7 copy-start.4
  33.4 32.9 %copy-start.1 = (bf16[128,2048]{1,0:T(8,128)(2,1)S(1)}, bf16[128,2048]{1,0:T(8,128)(2,1)}, u32[]{:S(2)}) copy-start(bf16[128,2048]{1,0:T(8,128)(2,1)} %shard_map.73.own_ref.refs_0_) | copy-start | bytes 1572868
  36.4 12.6 %collective-permute-start.9 = (bf16[128,2048]{1,0:T(8,128)(2,1)S(1)}, bf16[128,2048]{1,0:T(8,128)(2,1)S(1)}, u32[]{:S(2)}, u32[]{:S(2)}) collective-permute-start(bf16[128,2048]{1,0:T(8,128)(2,1)S(1)} %shard_map.75.refs_6_), channel_id=1, source_target_pairs={{0,2},{2,4},{4,6},{6,8},{8,10},{10,12},{12,14},{14,0},{1,15},{3,1}... | collective-permute-start | bytes 1572872 | tf_op jit(solution)/shard_map/ppermute | solution.py:269
  38.8 15.7 %collective-permute-start.3 = (bf16[128,2048]{1,0:T(8,128)(2,1)S(1)}, bf16[128,2048]{1,0:T(8,128)(2,1)S(1)}, u32[]{:S(2)}, u32[]{:S(2)}) collective-permute-start(bf16[128,2048]{1,0:T(8,128)(2,1)S(1)} %collective-permute-done.2.refs_2_), channel_id=1, source_target_pairs={{0,1},{1,0},{2,3},{3,2},{4,5},{5,4},{6,7},{7,6},{8,9},{9,8},{10,11... | collective-permute-start | bytes 1572872 | tf_op jit(solution)/shard_map/ppermute | solution.py:277
  42.2 14.2 %collective-permute-start.4 = (bf16[128,2048]{1,0:T(8,128)(2,1)S(1)}, bf16[128,2048]{1,0:T(8,128)(2,1)S(1)}, u32[]{:S(2)}, u32[]{:S(2)}) collective-permute-start(bf16[128,2048]{1,0:T(8,128)(2,1)S(1)} %collective-permute-done.1.got_ref.refs_4_), channel_id=1, source_target_pairs={{0,1},{1,0},{2,3},{3,2},{4,5},{5,4},{6,7},{7,6},{8,9},{9,8},{10,11... | collective-permute-start | bytes 1572872 | tf_op jit(solution)/shard_map/ppermute | solution.py:277
  44.1 14.7 %collective-permute-start.11 = (bf16[128,2048]{1,0:T(8,128)(2,1)S(1)}, bf16[128,2048]{1,0:T(8,128)(2,1)S(1)}, u32[]{:S(2)}, u32[]{:S(2)}) collective-permute-start(bf16[128,2048]{1,0:T(8,128)(2,1)S(1)} %collective-permute-done.7.refs_8_), channel_id=1, source_target_pairs={{0,2},{2,4},{4,6},{6,8},{8,10},{10,12},{12,14},{14,0},{1,15},{3,1}... | collective-permute-start | bytes 1572872 | tf_op jit(solution)/shard_map/ppermute | solution.py:269
  49.0 11.8 %collective-permute-start.13 = (bf16[128,2048]{1,0:T(8,128)(2,1)S(1)}, bf16[128,2048]{1,0:T(8,128)(2,1)S(1)}, u32[]{:S(2)}, u32[]{:S(2)}) collective-permute-start(bf16[128,2048]{1,0:T(8,128)(2,1)S(1)} %collective-permute-done.9.refs_10_), channel_id=1, source_target_pairs={{0,2},{2,4},{4,6},{6,8},{8,10},{10,12},{12,14},{14,0},{1,15},{3,1}... | collective-permute-start | bytes 1572872 | tf_op jit(solution)/shard_map/ppermute | solution.py:269
  51.0 13.8 %collective-permute-start.6 = (bf16[128,2048]{1,0:T(8,128)(2,1)S(1)}, bf16[128,2048]{1,0:T(8,128)(2,1)S(1)}, u32[]{:S(2)}, u32[]{:S(2)}) collective-permute-start(bf16[128,2048]{1,0:T(8,128)(2,1)S(1)} %shard_map.75.refs_6_), channel_id=1, source_target_pairs={{0,1},{1,0},{2,3},{3,2},{4,5},{5,4},{6,7},{7,6},{8,9},{9,8},{10,11... | collective-permute-start | bytes 1572872 | tf_op jit(solution)/shard_map/ppermute | solution.py:268
  54.5 10.3 %collective-permute-start.8 = (bf16[128,2048]{1,0:T(8,128)(2,1)S(1)}, bf16[128,2048]{1,0:T(8,128)(2,1)S(1)}, u32[]{:S(2)}, u32[]{:S(2)}) collective-permute-start(bf16[128,2048]{1,0:T(8,128)(2,1)S(1)} %collective-permute-done.7.refs_8_), channel_id=1, source_target_pairs={{0,1},{1,0},{2,3},{3,2},{4,5},{5,4},{6,7},{7,6},{8,9},{9,8},{10,11... | collective-permute-start | bytes 1572872 | tf_op jit(solution)/shard_map/ppermute | solution.py:277
  56.4 8.4 %collective-permute-start.10 = (bf16[128,2048]{1,0:T(8,128)(2,1)S(1)}, bf16[128,2048]{1,0:T(8,128)(2,1)S(1)}, u32[]{:S(2)}, u32[]{:S(2)}) collective-permute-start(bf16[128,2048]{1,0:T(8,128)(2,1)S(1)} %collective-permute-done.9.refs_10_), channel_id=1, source_target_pairs={{0,1},{1,0},{2,3},{3,2},{4,5},{5,4},{6,7},{7,6},{8,9},{9,8},{10,11... | collective-permute-start | bytes 1572872 | tf_op jit(solution)/shard_map/ppermute | solution.py:277
  58.8 6.0 %collective-permute-start.12 = (bf16[128,2048]{1,0:T(8,128)(2,1)S(1)}, bf16[128,2048]{1,0:T(8,128)(2,1)S(1)}, u32[]{:S(2)}, u32[]{:S(2)}) collective-permute-start(bf16[128,2048]{1,0:T(8,128)(2,1)S(1)} %collective-permute-done.11.refs_12_), channel_id=1, source_target_pairs={{0,1},{1,0},{2,3},{3,2},{4,5},{5,4},{6,7},{7,6},{8,9},{9,8},{10,11... | collective-permute-start | bytes 1572872 | tf_op jit(solution)/shard_map/ppermute | solution.py:277
  60.8 5.5 %collective-permute-start.14 = (bf16[128,2048]{1,0:T(8,128)(2,1)S(1)}, bf16[128,2048]{1,0:T(8,128)(2,1)S(1)}, u32[]{:S(2)}, u32[]{:S(2)}) collective-permute-start(bf16[128,2048]{1,0:T(8,128)(2,1)S(1)} %collective-permute-done.13.refs_14_), channel_id=1, source_target_pairs={{0,1},{1,0},{2,3},{3,2},{4,5},{5,4},{6,7},{7,6},{8,9},{9,8},{10,11... | collective-permute-start | bytes 1572872 | tf_op jit(solution)/shard_map/ppermute | solution.py:277

commit v3 on v2

--- a/solution.py
+++ b/solution.py
@@ -199,7 +199,7 @@
         pick(slot_ref[h], 0, len(NAMES), take)
         return carry
 
-    lax.fori_loop(0, HEADS, take_head, 0, unroll=4)
+    lax.fori_loop(0, HEADS, take_head, 0, unroll=32)
     ones = jnp.ones((2 * BLK, DH), jnp.bfloat16)
     for h in range(HEADS):
         g, cols = h // GROUP, head_columns(h)

time: 72.1 us -> 72.1 us (level)
  no operation moved by 1% of the time
where the time goes in v3:
time: 72.1 us; the launch traced here: 71.5 us
  starting transfers between devices  51.1 us (71%)
  Pallas kernels  10.1 us (14%)
  waiting for transfers between devices  6.21 us (9%)
  local copies, waits for them, and re-layouts  3.79 us (5%)
    ppermute x5, starting transfers between devices, shards(): last[lane] = lax.ppermute(last[lane], 'seq', RING)  16.1 us
    ppermute x6, starting transfers between devices, shards(): held['swp' + str(step) + lane] = lax.ppermute(last[lane], 'seq', SWAP)  15.6 us
    ppermute x2, starting transfers between devices, shards(): last[lane] = lax.ppermute(own, 'seq', RING if lane == 'A' else CROSS)  13.4 us
    pallas_call x1, Pallas kernels, far(): pl.pallas_call(far_kernel, out_shape=jax.ShapeDtypeStruct((BLK, HEADS * D...  5.14 us
    ppermute x2, waiting for transfers between devices, shards(): last[lane] = lax.ppermute(own, 'seq', RING if lane == 'A' else CROSS)  4.71 us
    unnamed x11, local copies, waits for them, and re-layouts  3.69 us
    ppermute x1, starting transfers between devices, shards(): held['swp2A'] = lax.ppermute(last[lane], 'seq', SWAP)  3.41 us
    pallas_call x1, Pallas kernels, near(): pl.pallas_call(near_kernel, out_shape=[jax.ShapeDtypeStruct((BLK, HEADS *...  2.96 us
  transfers between devices with their start and end apart: 15, of which 2 were waited for; matrix products, arithmetic and copies ran while one was open for 1% of the time, Pallas kernels for 4%

profile of v3, /device:TPU:1, one launch (start us, length us, event | category | flops | bytes accessed | tf_op | source)
XLA Modules:
  0.0 71.5 jit_solution(8949179507563970987)
XLA Ops:
  0.0 2.0 %shard_map.73.own_ref.refs_0_ = bf16[128,2048]{1,0:T(8,128)(2,1)} custom-call(bf16[128,512]{1,0:T(8,128)(2,1)} %refs_0_.1, bf16[128,512]{1,0:T(8,128)(2,1)} %refs_1_.1, bf16[128,512]{1,0:T(8,128)(2,1)} %refs_2_.1, bf16[128,512]{1,0:T(8,128)(2,1)} %refs_3_.1), custom_call_target="tpu_custom_call" | custom-call | bytes 1048576 | tf_op jit(solution)/shard_map/pallas_call | solution.py:83
  2.0 11.5 %collective-permute-start.2 = (bf16[128,2048]{1,0:T(8,128)(2,1)}, bf16[128,2048]{1,0:T(8,128)(2,1)S(1)}, u32[]{:S(2)}, u32[]{:S(2)}) collective-permute-start(bf16[128,2048]{1,0:T(8,128)(2,1)} %shard_map.73.own_ref.refs_0_), channel_id=1, source_target_pairs={{0,2},{2,4},{4,6},{6,8},{8,10},{10,12},{12,14},{14,0},{1,15},{3,1}... | collective-permute-start | bytes 1572872 | tf_op jit(solution)/shard_map/ppermute | solution.py:263
  13.5 1.9 %collective-permute-start.1 = (bf16[128,2048]{1,0:T(8,128)(2,1)}, bf16[128,2048]{1,0:T(8,128)(2,1)S(1)}, u32[]{:S(2)}, u32[]{:S(2)}) collective-permute-start(bf16[128,2048]{1,0:T(8,128)(2,1)} %shard_map.73.own_ref.refs_0_), channel_id=1, source_target_pairs={{1,2},{3,4},{5,6},{7,8},{9,10},{11,12},{13,14},{15,0},{0,15},{2,1}... | collective-permute-start | bytes 1572872 | tf_op jit(solution)/shard_map/ppermute | solution.py:263
  15.5 2.6 %collective-permute-start = (bf16[128,2048]{1,0:T(8,128)(2,1)}, bf16[128,2048]{1,0:T(8,128)(2,1)S(1)}, u32[]{:S(2)}, u32[]{:S(2)}) collective-permute-start(bf16[128,2048]{1,0:T(8,128)(2,1)} %shard_map.73.own_ref.refs_0_), channel_id=1, source_target_pairs={{0,1},{1,0},{2,3},{3,2},{4,5},{5,4},{6,7},{7,6},{8,9},{9,8},{10,11... | collective-permute-start | bytes 1572872 | tf_op jit(solution)/shard_map/ppermute | solution.py:272
  18.0 4.7 %collective-permute-done.2.refs_2_ = bf16[128,2048]{1,0:T(8,128)(2,1)S(1)} collective-permute-done((bf16[128,2048]{1,0:T(8,128)(2,1)}, bf16[128,2048]{1,0:T(8,128)(2,1)S(1)}, u32[]{:S(2)}, u32[]{:S(2)}) %collective-permute-start.2) | collective-permute-done | bytes 524320 | tf_op jit(solution)/shard_map/ppermute | solution.py:263
  22.7 4.9 %collective-permute-start.5 = (bf16[128,2048]{1,0:T(8,128)(2,1)S(1)}, bf16[128,2048]{1,0:T(8,128)(2,1)S(1)}, u32[]{:S(2)}, u32[]{:S(2)}) collective-permute-start(bf16[128,2048]{1,0:T(8,128)(2,1)S(1)} %collective-permute-done.2.refs_2_), channel_id=1, source_target_pairs={{0,2},{2,4},{4,6},{6,8},{8,10},{10,12},{12,14},{14,0},{1,15},{3,1}... | collective-permute-start | bytes 1572872 | tf_op jit(solution)/shard_map/ppermute | solution.py:269
  27.6 0.8 %copy.10 = s32[1,32,4]{2,1,0:T(8,128)S(1)} copy(s32[1,32,4]{1,2,0:T(4,128)} %param.12) | data formatting | bytes 1024 | tf_op args[5]
  28.5 1.9 %collective-permute-start.7 = (bf16[128,2048]{1,0:T(8,128)(2,1)S(1)}, bf16[128,2048]{1,0:T(8,128)(2,1)S(1)}, u32[]{:S(2)}, u32[]{:S(2)}) collective-permute-start(bf16[128,2048]{1,0:T(8,128)(2,1)S(1)} %collective-permute-done.1.got_ref.refs_4_), channel_id=1, source_target_pairs={{0,2},{2,4},{4,6},{6,8},{8,10},{10,12},{12,14},{14,0},{1,15},{3,1}... | collective-permute-start | bytes 1572872 | tf_op jit(solution)/shard_map/ppermute | solution.py:269
  30.5 1.0 %copy-done = bf16[128,2048]{1,0:T(8,128)(2,1)S(1)} copy-done((bf16[128,2048]{1,0:T(8,128)(2,1)S(1)}, bf16[128,2048]{1,0:T(8,128)(2,1)}, u32[]{:S(2)}) %copy-start) | copy-done | bytes 524312
  31.5 1.2 %copy-done.2 = bf16[128,4096]{1,0:T(8,128)(2,1)S(1)} copy-done((bf16[128,4096]{1,0:T(8,128)(2,1)S(1)}, bf16[128,4096]{1,0:T(8,128)(2,1)}, u32[]{:S(2)}) %copy-start.2) | copy-done | bytes 1048600
  32.8 0.7 copy-done.4
  33.4 3.0 %shard_map.74 = (f32[128,4096]{1,0:T(8,128)S(1)}, f32[128,4096]{1,0:T(8,128)S(1)}, f32[128,4096]{1,0:T(8,128)S(1)}, s32[32]{0:T(128)S(1)}, s32[32]{0:T(128)S(1)}) custom-call(s32[1]{0:T(128)} %bitcast.me_ref, s32[32]{0:T(128)S(1)} %copy-done.4, s32[128]{0:T(128)S(1)} %reshape.7.lists_ref, bf16[128,4096]{1,0:T(8,128)(2,1)S(1)} %copy-done.2, ...), custom_call_target="tpu_custom_call" | custom-call | flops 536870912 | bytes 4194304 | tf_op jit(solution)/shard_map/pallas_call | solution.py:160
  36.4 2.4 %collective-permute-start.9 = (bf16[128,2048]{1,0:T(8,128)(2,1)S(1)}, bf16[128,2048]{1,0:T(8,128)(2,1)S(1)}, u32[]{:S(2)}, u32[]{:S(2)}) collective-permute-start(bf16[128,2048]{1,0:T(8,128)(2,1)S(1)} %shard_map.75.refs_6_), channel_id=1, source_target_pairs={{0,2},{2,4},{4,6},{6,8},{8,10},{10,12},{12,14},{14,0},{1,15},{3,1}... | collective-permute-start | bytes 1572872 | tf_op jit(solution)/shard_map/ppermute | solution.py:269
  38.8 3.4 %collective-permute-start.3 = (bf16[128,2048]{1,0:T(8,128)(2,1)S(1)}, bf16[128,2048]{1,0:T(8,128)(2,1)S(1)}, u32[]{:S(2)}, u32[]{:S(2)}) collective-permute-start(bf16[128,2048]{1,0:T(8,128)(2,1)S(1)} %collective-permute-done.2.refs_2_), channel_id=1, source_target_pairs={{0,1},{1,0},{2,3},{3,2},{4,5},{5,4},{6,7},{7,6},{8,9},{9,8},{10,11... | collective-permute-start | bytes 1572872 | tf_op jit(solution)/shard_map/ppermute | solution.py:277
  42.2 1.9 %collective-permute-start.4 = (bf16[128,2048]{1,0:T(8,128)(2,1)S(1)}, bf16[128,2048]{1,0:T(8,128)(2,1)S(1)}, u32[]{:S(2)}, u32[]{:S(2)}) collective-permute-start(bf16[128,2048]{1,0:T(8,128)(2,1)S(1)} %collective-permute-done.1.got_ref.refs_4_), channel_id=1, source_target_pairs={{0,1},{1,0},{2,3},{3,2},{4,5},{5,4},{6,7},{7,6},{8,9},{9,8},{10,11... | collective-permute-start | bytes 1572872 | tf_op jit(solution)/shard_map/ppermute | solution.py:277
  44.1 4.9 %collective-permute-start.11 = (bf16[128,2048]{1,0:T(8,128)(2,1)S(1)}, bf16[128,2048]{1,0:T(8,128)(2,1)S(1)}, u32[]{:S(2)}, u32[]{:S(2)}) collective-permute-start(bf16[128,2048]{1,0:T(8,128)(2,1)S(1)} %collective-permute-done.7.refs_8_), channel_id=1, source_target_pairs={{0,2},{2,4},{4,6},{6,8},{8,10},{10,12},{12,14},{14,0},{1,15},{3,1}... | collective-permute-start | bytes 1572872 | tf_op jit(solution)/shard_map/ppermute | solution.py:269
  49.0 2.0 %collective-permute-start.13 = (bf16[128,2048]{1,0:T(8,128)(2,1)S(1)}, bf16[128,2048]{1,0:T(8,128)(2,1)S(1)}, u32[]{:S(2)}, u32[]{:S(2)}) collective-permute-start(bf16[128,2048]{1,0:T(8,128)(2,1)S(1)} %collective-permute-done.9.refs_10_), channel_id=1, source_target_pairs={{0,2},{2,4},{4,6},{6,8},{8,10},{10,12},{12,14},{14,0},{1,15},{3,1}... | collective-permute-start | bytes 1572872 | tf_op jit(solution)/shard_map/ppermute | solution.py:269
  51.0 3.4 %collective-permute-start.6 = (bf16[128,2048]{1,0:T(8,128)(2,1)S(1)}, bf16[128,2048]{1,0:T(8,128)(2,1)S(1)}, u32[]{:S(2)}, u32[]{:S(2)}) collective-permute-start(bf16[128,2048]{1,0:T(8,128)(2,1)S(1)} %shard_map.75.refs_6_), channel_id=1, source_target_pairs={{0,1},{1,0},{2,3},{3,2},{4,5},{5,4},{6,7},{7,6},{8,9},{9,8},{10,11... | collective-permute-start | bytes 1572872 | tf_op jit(solution)/shard_map/ppermute | solution.py:268
  54.5 1.9 %collective-permute-start.8 = (bf16[128,2048]{1,0:T(8,128)(2,1)S(1)}, bf16[128,2048]{1,0:T(8,128)(2,1)S(1)}, u32[]{:S(2)}, u32[]{:S(2)}) collective-permute-start(bf16[128,2048]{1,0:T(8,128)(2,1)S(1)} %collective-permute-done.7.refs_8_), channel_id=1, source_target_pairs={{0,1},{1,0},{2,3},{3,2},{4,5},{5,4},{6,7},{7,6},{8,9},{9,8},{10,11... | collective-permute-start | bytes 1572872 | tf_op jit(solution)/shard_map/ppermute | solution.py:277
  56.4 2.4 %collective-permute-start.10 = (bf16[128,2048]{1,0:T(8,128)(2,1)S(1)}, bf16[128,2048]{1,0:T(8,128)(2,1)S(1)}, u32[]{:S(2)}, u32[]{:S(2)}) collective-permute-start(bf16[128,2048]{1,0:T(8,128)(2,1)S(1)} %collective-permute-done.9.refs_10_), channel_id=1, source_target_pairs={{0,1},{1,0},{2,3},{3,2},{4,5},{5,4},{6,7},{7,6},{8,9},{9,8},{10,11... | collective-permute-start | bytes 1572872 | tf_op jit(solution)/shard_map/ppermute | solution.py:277
  58.8 1.9 %collective-permute-start.12 = (bf16[128,2048]{1,0:T(8,128)(2,1)S(1)}, bf16[128,2048]{1,0:T(8,128)(2,1)S(1)}, u32[]{:S(2)}, u32[]{:S(2)}) collective-permute-start(bf16[128,2048]{1,0:T(8,128)(2,1)S(1)} %collective-permute-done.11.refs_12_), channel_id=1, source_target_pairs={{0,1},{1,0},{2,3},{3,2},{4,5},{5,4},{6,7},{7,6},{8,9},{9,8},{10,11... | collective-permute-start | bytes 1572872 | tf_op jit(solution)/shard_map/ppermute | solution.py:277
  60.8 4.0 %collective-permute-start.14 = (bf16[128,2048]{1,0:T(8,128)(2,1)S(1)}, bf16[128,2048]{1,0:T(8,128)(2,1)S(1)}, u32[]{:S(2)}, u32[]{:S(2)}) collective-permute-start(bf16[128,2048]{1,0:T(8,128)(2,1)S(1)} %collective-permute-done.13.refs_14_), channel_id=1, source_target_pairs={{0,1},{1,0},{2,3},{3,2},{4,5},{5,4},{6,7},{7,6},{8,9},{9,8},{10,11... | collective-permute-start | bytes 1572872 | tf_op jit(solution)/shard_map/ppermute | solution.py:277
  64.8 1.5 %collective-permute-done.14.refs_15_ = bf16[128,2048]{1,0:T(8,128)(2,1)S(1)} collective-permute-done((bf16[128,2048]{1,0:T(8,128)(2,1)S(1)}, bf16[128,2048]{1,0:T(8,128)(2,1)S(1)}, u32[]{:S(2)}, u32[]{:S(2)}) %collective-permute-start.14) | collective-permute-done | bytes 524320 | tf_op jit(solution)/shard_map/ppermute | solution.py:277
  66.3 5.1 %shard_map.76 = bf16[128,4096]{1,0:T(8,128)(2,1)} custom-call(s32[1]{0:T(128)} %bitcast.me_ref, s32[32]{0:T(128)S(1)} %copy-done.4, s32[32]{0:T(128)S(1)} %get-tuple-element.10.after.slot_ref, s32[32]{0:T(128)S(1)} %get-tuple-element.11.half_ref, bf16[128,4096]{1,0:T(8,128)(2,1)S(1)} %copy-done.3, f32[128,4096]{1,0:T(8,128)S(1)} %get-tuple-element.12.total_ref, ...), custom_call_target="tpu_custom_call" | custom-call | flops 536870912 | bytes 6291456 | tf_op jit(solution)/shard_map/pallas_call | solution.py:237
  (22 shorter events, 0.2 us)
Async XLA Ops:
  0.0 66.3 %copy-start.3 = (bf16[128,4096]{1,0:T(8,128)(2,1)S(1)}, bf16[128,4096]{1,0:T(8,128)(2,1)}, u32[]{:S(2)}) copy-start(bf16[128,4096]{1,0:T(8,128)(2,1)} %q_ref.3) | copy-start | bytes 3145732
  2.0 20.7 %collective-permute-start.2 = (bf16[128,2048]{1,0:T(8,128)(2,1)}, bf16[128,2048]{1,0:T(8,128)(2,1)S(1)}, u32[]{:S(2)}, u32[]{:S(2)}) collective-permute-start(bf16[128,2048]{1,0:T(8,128)(2,1)} %shard_map.73.own_ref.refs_0_), channel_id=1, source_target_pairs={{0,2},{2,4},{4,6},{6,8},{8,10},{10,12},{12,14},{14,0},{1,15},{3,1}... | collective-permute-start | bytes 1572872 | tf_op jit(solution)/shard_map/ppermute | solution.py:263
  13.5 15.0 %collective-permute-start.1 = (bf16[128,2048]{1,0:T(8,128)(2,1)}, bf16[128,2048]{1,0:T(8,128)(2,1)S(1)}, u32[]{:S(2)}, u32[]{:S(2)}) collective-permute-start(bf16[128,2048]{1,0:T(8,128)(2,1)} %shard_map.73.own_ref.refs_0_), channel_id=1, source_target_pairs={{1,2},{3,4},{5,6},{7,8},{9,10},{11,12},{13,14},{15,0},{0,15},{2,1}... | collective-permute-start | bytes 1572872 | tf_op jit(solution)/shard_map/ppermute | solution.py:263
  15.5 15.0 %collective-permute-start = (bf16[128,2048]{1,0:T(8,128)(2,1)}, bf16[128,2048]{1,0:T(8,128)(2,1)S(1)}, u32[]{:S(2)}, u32[]{:S(2)}) collective-permute-start(bf16[128,2048]{1,0:T(8,128)(2,1)} %shard_map.73.own_ref.refs_0_), channel_id=1, source_target_pairs={{0,1},{1,0},{2,3},{3,2},{4,5},{5,4},{6,7},{7,6},{8,9},{9,8},{10,11... | collective-permute-start | bytes 1572872 | tf_op jit(solution)/shard_map/ppermute | solution.py:272
  22.7 13.7 %collective-permute-start.5 = (bf16[128,2048]{1,0:T(8,128)(2,1)S(1)}, bf16[128,2048]{1,0:T(8,128)(2,1)S(1)}, u32[]{:S(2)}, u32[]{:S(2)}) collective-permute-start(bf16[128,2048]{1,0:T(8,128)(2,1)S(1)} %collective-permute-done.2.refs_2_), channel_id=1, source_target_pairs={{0,2},{2,4},{4,6},{6,8},{8,10},{10,12},{12,14},{14,0},{1,15},{3,1}... | collective-permute-start | bytes 1572872 | tf_op jit(solution)/shard_map/ppermute | solution.py:269
  28.5 15.6 %collective-permute-start.7 = (bf16[128,2048]{1,0:T(8,128)(2,1)S(1)}, bf16[128,2048]{1,0:T(8,128)(2,1)S(1)}, u32[]{:S(2)}, u32[]{:S(2)}) collective-permute-start(bf16[128,2048]{1,0:T(8,128)(2,1)S(1)} %collective-permute-done.1.got_ref.refs_4_), channel_id=1, source_target_pairs={{0,2},{2,4},{4,6},{6,8},{8,10},{10,12},{12,14},{14,0},{1,15},{3,1}... | collective-permute-start | bytes 1572872 | tf_op jit(solution)/shard_map/ppermute | solution.py:269
  30.5 1.0 %copy-start = (bf16[128,2048]{1,0:T(8,128)(2,1)S(1)}, bf16[128,2048]{1,0:T(8,128)(2,1)}, u32[]{:S(2)}) copy-start(bf16[128,2048]{1,0:T(8,128)(2,1)} %shard_map.73.own_ref.refs_0_) | copy-start | bytes 1572868
  31.5 1.2 %copy-start.2 = (bf16[128,4096]{1,0:T(8,128)(2,1)S(1)}, bf16[128,4096]{1,0:T(8,128)(2,1)}, u32[]{:S(2)}) copy-start(bf16[128,4096]{1,0:T(8,128)(2,1)} %q_ref.3) | copy-start | bytes 3145732
  32.8 0.7 copy-start.4
  33.4 32.9 %copy-start.1 = (bf16[128,2048]{1,0:T(8,128)(2,1)S(1)}, bf16[128,2048]{1,0:T(8,128)(2,1)}, u32[]{:S(2)}) copy-start(bf16[128,2048]{1,0:T(8,128)(2,1)} %shard_map.73.own_ref.refs_0_) | copy-start | bytes 1572868
  36.4 12.6 %collective-permute-start.9 = (bf16[128,2048]{1,0:T(8,128)(2,1)S(1)}, bf16[128,2048]{1,0:T(8,128)(2,1)S(1)}, u32[]{:S(2)}, u32[]{:S(2)}) collective-permute-start(bf16[128,2048]{1,0:T(8,128)(2,1)S(1)} %shard_map.75.refs_6_), channel_id=1, source_target_pairs={{0,2},{2,4},{4,6},{6,8},{8,10},{10,12},{12,14},{14,0},{1,15},{3,1}... | collective-permute-start | bytes 1572872 | tf_op jit(solution)/shard_map/ppermute | solution.py:269
  38.8 15.7 %collective-permute-start.3 = (bf16[128,2048]{1,0:T(8,128)(2,1)S(1)}, bf16[128,2048]{1,0:T(8,128)(2,1)S(1)}, u32[]{:S(2)}, u32[]{:S(2)}) collective-permute-start(bf16[128,2048]{1,0:T(8,128)(2,1)S(1)} %collective-permute-done.2.refs_2_), channel_id=1, source_target_pairs={{0,1},{1,0},{2,3},{3,2},{4,5},{5,4},{6,7},{7,6},{8,9},{9,8},{10,11... | collective-permute-start | bytes 1572872 | tf_op jit(solution)/shard_map/ppermute | solution.py:277
  42.2 14.2 %collective-permute-start.4 = (bf16[128,2048]{1,0:T(8,128)(2,1)S(1)}, bf16[128,2048]{1,0:T(8,128)(2,1)S(1)}, u32[]{:S(2)}, u32[]{:S(2)}) collective-permute-start(bf16[128,2048]{1,0:T(8,128)(2,1)S(1)} %collective-permute-done.1.got_ref.refs_4_), channel_id=1, source_target_pairs={{0,1},{1,0},{2,3},{3,2},{4,5},{5,4},{6,7},{7,6},{8,9},{9,8},{10,11... | collective-permute-start | bytes 1572872 | tf_op jit(solution)/shard_map/ppermute | solution.py:277
  44.1 14.7 %collective-permute-start.11 = (bf16[128,2048]{1,0:T(8,128)(2,1)S(1)}, bf16[128,2048]{1,0:T(8,128)(2,1)S(1)}, u32[]{:S(2)}, u32[]{:S(2)}) collective-permute-start(bf16[128,2048]{1,0:T(8,128)(2,1)S(1)} %collective-permute-done.7.refs_8_), channel_id=1, source_target_pairs={{0,2},{2,4},{4,6},{6,8},{8,10},{10,12},{12,14},{14,0},{1,15},{3,1}... | collective-permute-start | bytes 1572872 | tf_op jit(solution)/shard_map/ppermute | solution.py:269
  49.0 11.8 %collective-permute-start.13 = (bf16[128,2048]{1,0:T(8,128)(2,1)S(1)}, bf16[128,2048]{1,0:T(8,128)(2,1)S(1)}, u32[]{:S(2)}, u32[]{:S(2)}) collective-permute-start(bf16[128,2048]{1,0:T(8,128)(2,1)S(1)} %collective-permute-done.9.refs_10_), channel_id=1, source_target_pairs={{0,2},{2,4},{4,6},{6,8},{8,10},{10,12},{12,14},{14,0},{1,15},{3,1}... | collective-permute-start | bytes 1572872 | tf_op jit(solution)/shard_map/ppermute | solution.py:269
  51.0 13.8 %collective-permute-start.6 = (bf16[128,2048]{1,0:T(8,128)(2,1)S(1)}, bf16[128,2048]{1,0:T(8,128)(2,1)S(1)}, u32[]{:S(2)}, u32[]{:S(2)}) collective-permute-start(bf16[128,2048]{1,0:T(8,128)(2,1)S(1)} %shard_map.75.refs_6_), channel_id=1, source_target_pairs={{0,1},{1,0},{2,3},{3,2},{4,5},{5,4},{6,7},{7,6},{8,9},{9,8},{10,11... | collective-permute-start | bytes 1572872 | tf_op jit(solution)/shard_map/ppermute | solution.py:268
  54.5 10.3 %collective-permute-start.8 = (bf16[128,2048]{1,0:T(8,128)(2,1)S(1)}, bf16[128,2048]{1,0:T(8,128)(2,1)S(1)}, u32[]{:S(2)}, u32[]{:S(2)}) collective-permute-start(bf16[128,2048]{1,0:T(8,128)(2,1)S(1)} %collective-permute-done.7.refs_8_), channel_id=1, source_target_pairs={{0,1},{1,0},{2,3},{3,2},{4,5},{5,4},{6,7},{7,6},{8,9},{9,8},{10,11... | collective-permute-start | bytes 1572872 | tf_op jit(solution)/shard_map/ppermute | solution.py:277
  56.4 8.4 %collective-permute-start.10 = (bf16[128,2048]{1,0:T(8,128)(2,1)S(1)}, bf16[128,2048]{1,0:T(8,128)(2,1)S(1)}, u32[]{:S(2)}, u32[]{:S(2)}) collective-permute-start(bf16[128,2048]{1,0:T(8,128)(2,1)S(1)} %collective-permute-done.9.refs_10_), channel_id=1, source_target_pairs={{0,1},{1,0},{2,3},{3,2},{4,5},{5,4},{6,7},{7,6},{8,9},{9,8},{10,11... | collective-permute-start | bytes 1572872 | tf_op jit(solution)/shard_map/ppermute | solution.py:277
  58.8 6.0 %collective-permute-start.12 = (bf16[128,2048]{1,0:T(8,128)(2,1)S(1)}, bf16[128,2048]{1,0:T(8,128)(2,1)S(1)}, u32[]{:S(2)}, u32[]{:S(2)}) collective-permute-start(bf16[128,2048]{1,0:T(8,128)(2,1)S(1)} %collective-permute-done.11.refs_12_), channel_id=1, source_target_pairs={{0,1},{1,0},{2,3},{3,2},{4,5},{5,4},{6,7},{7,6},{8,9},{9,8},{10,11... | collective-permute-start | bytes 1572872 | tf_op jit(solution)/shard_map/ppermute | solution.py:277
  60.8 5.5 %collective-permute-start.14 = (bf16[128,2048]{1,0:T(8,128)(2,1)S(1)}, bf16[128,2048]{1,0:T(8,128)(2,1)S(1)}, u32[]{:S(2)}, u32[]{:S(2)}) collective-permute-start(bf16[128,2048]{1,0:T(8,128)(2,1)S(1)} %collective-permute-done.13.refs_14_), channel_id=1, source_target_pairs={{0,1},{1,0},{2,3},{3,2},{4,5},{5,4},{6,7},{7,6},{8,9},{9,8},{10,11... | collective-permute-start | bytes 1572872 | tf_op jit(solution)/shard_map/ppermute | solution.py:277

commit v4 on v3

--- a/solution.py
+++ b/solution.py
@@ -26,30 +26,30 @@
 ]
 SWAP = [(i, i ^ 1) for i in range(SEQ)]
 
-NAMES = ["own", "oth"] + [
-    kind + str(step) + lane
-    for step in (1, 2, 3, 4)
-    for lane in ("A", "B")
-    for kind in ("got", "swp")
-    if (step, lane) != (4, "B")
-]
-
-
-def slot_table():
-    table = np.zeros((2, CHIPS, 2), np.int32)
-    for core in range(2):
-        for away in range(CHIPS):
-            for owner in range(2):
-                if away == 0:
-                    name = "own" if owner == core else "oth"
-                else:
-                    down = away < 4 or (away == 4 and owner == 1)
-                    step = away if down else CHIPS - away
-                    lane = "A" if owner == (1 if down else 0) else "B"
-                    kind = "got" if core == (1 if down else 0) else "swp"
-                    name = kind + str(step) + lane
-                table[core, away, owner] = NAMES.index(name)
-    return table
+RING_LATE = [(source, target) for source, target in RING if source < target and source >= SEQ // 2 - 2 and source % 2 == 0]
+SHARE_LATE = [(target, target + 1) for source, target in RING_LATE]
+
+NAMES = ["own", "oth"] + [kind + step for step in ("1", "2", "3", "4C", "4S") for kind in ("g", "s")]
+COLUMNS = 40
+
+
+def place_table():
+    table = np.zeros((2, 2, 2, CHIPS, 2), np.int32)
+    for part, core, away, owner in np.ndindex(*table.shape[1:]):
+        column = 2 * WIDTH * part
+        if away == 0:
+            name = "own" if owner == core else "oth"
+        else:
+            down = away < 4 or (away == 4 and owner == 1)
+            step = away if down else CHIPS - away
+            lane_b = owner != (1 if down else 0)
+            name = ("g" if core == (1 if down else 0) else "s") + str(step)
+            if step < 4:
+                column += 4 * WIDTH * lane_b
+            else:
+                name, column = ("gs"[core] + "4S", 2 * WIDTH * owner) if part else (name + "C", 0)
+        table[:, part, core, away, owner] = NAMES.index(name), column
+    return table.reshape(-1)
 
 
 def pick(slot, low, high, use):
@@ -104,7 +104,7 @@
 
 
 def near_kernel(
-    me_ref, table_ref, lists_ref, q_ref, own_ref, oth_ref, got_ref, total_ref, sum_ref, top_ref, slot_ref, half_ref, new, old, sems
+    me_ref, table_ref, lists_ref, q_ref, own_ref, oth_ref, got_ref, total_ref, sum_ref, top_ref, place_ref, new, old, sems
 ):
     me = me_ref[0]
     core = lax.rem(me, 2)
@@ -123,16 +123,20 @@
     def _():
         old_copy(got_ref).start()
 
+    def place(n, block, column):
+        owner = lax.rem(block, SEQ)
+        away = lax.rem(owner // 2 - me // 2 + CHIPS, CHIPS)
+        entry = block // SEQ * 4 * CHIPS + core * 2 * CHIPS + away * 2 + lax.rem(owner, 2)
+        place_ref[n] = table_ref[entry]
+        place_ref[COLUMNS + n] = table_ref[8 * CHIPS + entry] + column
+
     def locate(h, carry):
         chosen = lists_ref[4 * h] + lists_ref[4 * h + 1] + lists_ref[4 * h + 2] + lists_ref[4 * h + 3]
-        chosen = jnp.clip(chosen - (2 * (SEQ + me) - 1), 0, 2 * SEQ - 1)
-        owner = lax.rem(chosen, SEQ)
-        away = lax.rem(owner // 2 - me // 2 + CHIPS, CHIPS)
-        slot_ref[h] = table_ref[core * 2 * CHIPS + away * 2 + lax.rem(owner, 2)]
-        half_ref[h] = chosen // SEQ
+        place(h, jnp.clip(chosen - (2 * (SEQ + me) - 1), 0, 2 * SEQ - 1), h // GROUP * DH)
         return carry
 
     lax.fori_loop(0, HEADS, locate, 0)
+    place(HEADS, jnp.int32(0), 0)
     own_copy.wait()
     old_copy(oth_ref).wait()
 
@@ -163,11 +167,10 @@
             jax.ShapeDtypeStruct((BLK, HEADS * DH), jnp.float32),
             jax.ShapeDtypeStruct((BLK, HEADS * DH), jnp.float32),
             jax.ShapeDtypeStruct((BLK, HEADS * DH), jnp.float32),
-            jax.ShapeDtypeStruct((HEADS,), jnp.int32),
-            jax.ShapeDtypeStruct((HEADS,), jnp.int32),
+            jax.ShapeDtypeStruct((2 * COLUMNS,), jnp.int32),
         ],
         in_specs=[smem] * 3 + [vmem] + [anywhere] * 3,
-        out_specs=[vmem, vmem, vmem, smem, smem],
+        out_specs=[vmem, vmem, vmem, smem],
         scratch_shapes=[
             pltpu.VMEM((BLK, 2 * WIDTH), jnp.bfloat16),
             pltpu.VMEM((BLK, 2 * WIDTH), jnp.bfloat16),
@@ -178,25 +181,24 @@
     )(me, table, lists, queries, own, oth, got)
 
 
-def far_kernel(me_ref, table_ref, slot_ref, half_ref, q_ref, total_ref, sum_ref, top_ref, *refs):
+def far_kernel(place_ref, q_ref, total_ref, sum_ref, top_ref, *refs):
     held = refs[: len(NAMES)]
     o_ref, first, k_pick, v_pick = refs[len(NAMES) :]
-    me = me_ref[0]
-    slot = table_ref[lax.rem(me, 2) * 2 * CHIPS + lax.rem(CHIPS - me // 2, CHIPS) * 2]
+    first_column = pl.multiple_of(place_ref[COLUMNS + HEADS], DH)
 
     def take_first(b):
-        first[...] = held[b][:, : 2 * WIDTH]
-
-    pick(slot, 0, len(NAMES), take_first)
+        first[...] = held[b][:, pl.ds(first_column, 2 * WIDTH)]
+
+    pick(place_ref[HEADS], 0, len(NAMES), take_first)
 
     def take_head(h, carry):
-        column = pl.multiple_of(half_ref[h] * 2 * WIDTH + (h // GROUP) * DH, DH)
+        column = pl.multiple_of(place_ref[COLUMNS + h], DH)
 
         def take(b):
             k_pick[h] = held[b][:, pl.ds(column, DH)]
             v_pick[h] = held[b][:, pl.ds(column + WIDTH, DH)]
 
-        pick(slot_ref[h], 0, len(NAMES), take)
+        pick(place_ref[h], 0, len(NAMES), take)
         return carry
 
     lax.fori_loop(0, HEADS, take_head, 0, unroll=32)
@@ -221,7 +223,7 @@
     pass
 
 
-def tie(through, after):
+def tie(through, after, flops=0):
     return pl.pallas_call(
         tie_kernel,
         out_shape=jax.ShapeDtypeStruct(through.shape, through.dtype),
@@ -229,15 +231,16 @@
         out_specs=pl.BlockSpec(memory_space=pl.ANY),
         input_output_aliases={0: 0},
         compiler_params=pltpu.CompilerParams(vmem_limit_bytes=1 << 20),
+        cost_estimate=pl.CostEstimate(flops=flops, bytes_accessed=0, transcendentals=0),
     )(through, after)
 
 
-def far(me, table, slots, halves, queries, near_parts, held):
+def far(places, queries, near_parts, held):
     smem, vmem = pl.BlockSpec(memory_space=pltpu.SMEM), pl.BlockSpec(memory_space=pltpu.VMEM)
     return pl.pallas_call(
         far_kernel,
         out_shape=jax.ShapeDtypeStruct((BLK, HEADS * DH), jnp.bfloat16),
-        in_specs=[smem] * 4 + [vmem] * (4 + len(NAMES)),
+        in_specs=[smem] + [vmem] * (4 + len(NAMES)),
         out_specs=vmem,
         scratch_shapes=[
             pltpu.VMEM((BLK, 2 * WIDTH), jnp.bfloat16),
@@ -246,36 +249,34 @@
         ],
         compiler_params=pltpu.CompilerParams(vmem_limit_bytes=24 << 20),
         cost_estimate=pl.CostEstimate(flops=1 << 29, bytes_accessed=6 << 20, transcendentals=1 << 20),
-    )(me, table, slots, halves, queries, *near_parts, *held)
+    )(places, queries, *near_parts, *held)
 
 
 def shards(queries, span_keys, span_values, cache_keys, cache_values, block_lists):
     me = lax.axis_index("seq").astype(jnp.int32).reshape(1)
-    table = jnp.asarray(slot_table().reshape(-1))
-    own = join([cache_keys, cache_values, span_keys, span_values])
-    held = {"own": own}
-    last = {}
-    for step in (1, 2, 3, 4):
-        for lane in ("A", "B"):
-            if (step, lane) == (4, "B"):
-                continue
-            if step == 1:
-                last[lane] = lax.ppermute(own, "seq", RING if lane == "A" else CROSS)
-            else:
-                if (step, lane) == (3, "A"):
-                    last[lane] = tie(last[lane], slots)
-                    held["got2A"] = last[lane]
-                    held["swp2A"] = lax.ppermute(last[lane], "seq", SWAP)
-                last[lane] = lax.ppermute(last[lane], "seq", RING)
-            held["got" + str(step) + lane] = last[lane]
-            if (step, lane) == (1, "B"):
-                held["oth"] = lax.ppermute(own, "seq", SWAP)
-                total, sums, tops, slots, halves = near(
-                    me, table, block_lists.reshape(-1), queries, own, held["oth"], held["got1B"]
-                )
-            if (step, lane) != (2, "A"):
-                held["swp" + str(step) + lane] = lax.ppermute(last[lane], "seq", SWAP)
-    return far(me, table, slots, halves, queries, (total, sums, tops), [held[name] for name in NAMES])
+    table = jnp.asarray(place_table())
+
+    def send(x, pairs):
+        return lax.ppermute(x, "seq", pairs)
+
+    held = {"own": join([cache_keys, cache_values, span_keys, span_values])}
+    lane_a, lane_b = send(held["own"], RING), send(held["own"], CROSS)
+    held["oth"] = send(held["own"], SWAP)
+    *near_parts, places = near(me, table, block_lists.reshape(-1), queries, held["own"], held["oth"], lane_b)
+    held["g1"] = jnp.concatenate([lane_a, lane_b], axis=1)
+    lane_a, lane_b = tie(send(lane_a, RING), places), send(lane_b, RING)
+    held["g2"] = jnp.concatenate([lane_a, lane_b], axis=1)
+    lane_a, lane_b = send(lane_a, RING), send(lane_b, RING)
+    held["g3"] = jnp.concatenate([lane_a, lane_b], axis=1)
+    for name in ("1", "2", "3"):
+        held["s" + name] = send(held["g" + name], SWAP)
+    held["g4C"] = send(lane_a[:, : 2 * WIDTH], RING)
+    held["s4C"] = send(tie(tie(held["g4C"], places, 1 << 34), held["s3"]), SWAP)
+    held["g4S"] = send(jnp.concatenate([lane_a[:, 2 * WIDTH :], lane_b[:, 2 * WIDTH :]], axis=1), RING_LATE)
+    held["s4S"] = send(held["g4S"], SHARE_LATE)
+    held["s2"] = tie(held["s2"], places, 1 << 33)
+    held["s4S"] = tie(held["s4S"], places, 1 << 33)
+    return far(places, queries, near_parts, [held[name] for name in NAMES])
 
 
 def solution(mesh):

time: 72.1 us -> 72.2 us (level)
  the two profiles are of different devices: /device:TPU:1 before, /device:TPU:285 now
where the time goes in v4:
time: 72.2 us; the launch traced here: 71.6 us
  starting transfers between devices  49.7 us (69%)
  Pallas kernels  10.1 us (14%)
  waiting for transfers between devices  7.23 us (10%)
  local copies, waits for them, and re-layouts  4.01 us (6%)
    ppermute x14, starting transfers between devices, send(): return lax.ppermute(x, 'seq', pairs)  49.7 us
    ppermute x14, waiting for transfers between devices, send(): return lax.ppermute(x, 'seq', pairs)  7.23 us
    pallas_call x1, Pallas kernels, far(): pl.pallas_call(far_kernel, out_shape=jax.ShapeDtypeStruct((BLK, HEADS * D...  5.22 us
    unnamed x14, local copies, waits for them, and re-layouts  3.78 us
    pallas_call x1, Pallas kernels, near(): pl.pallas_call(near_kernel, out_shape=[jax.ShapeDtypeStruct((BLK, HEADS *...  2.99 us
    pallas_call x1, Pallas kernels, join(): pl.pallas_call(join_kernel, out_shape=jax.ShapeDtypeStruct((BLK, 4 * WIDT...  1.92 us
  transfers between devices with their start and end apart: 14, of which 5 were waited for; matrix products, arithmetic and copies ran while one was open for 2% of the time, Pallas kernels for 4%

profile of v4, /device:TPU:285, one launch (start us, length us, event | category | flops | bytes accessed | tf_op | source)
XLA Modules:
  0.0 71.6 jit_solution(16541862088401860705)
XLA Ops:
  0.0 1.9 %shard_map.73.own_ref.refs_0_ = bf16[128,2048]{1,0:T(8,128)(2,1)} custom-call(bf16[128,512]{1,0:T(8,128)(2,1)} %refs_0_.1, bf16[128,512]{1,0:T(8,128)(2,1)} %refs_1_.1, bf16[128,512]{1,0:T(8,128)(2,1)} %refs_2_.1, bf16[128,512]{1,0:T(8,128)(2,1)} %refs_3_.1), custom_call_target="tpu_custom_call" | custom-call | bytes 1048576 | tf_op jit(solution)/shard_map/pallas_call | solution.py:83
  1.9 1.9 %collective-permute-start.2 = (bf16[128,2048]{1,0:T(8,128)(2,1)}, bf16[128,2048]{1,0:T(8,128)(2,1)S(1)}, u32[]{:S(2)}, u32[]{:S(2)}) collective-permute-start(bf16[128,2048]{1,0:T(8,128)(2,1)} %shard_map.73.own_ref.refs_0_), channel_id=1, source_target_pairs={{0,2},{2,4},{4,6},{6,8},{8,10},{10,12},{12,14},{14,0},{1,15},{3,1}... | collective-permute-start | bytes 1572872 | tf_op jit(solution)/shard_map/ppermute | solution.py:260
  3.9 5.1 %collective-permute-start.1 = (bf16[128,2048]{1,0:T(8,128)(2,1)}, bf16[128,2048]{1,0:T(8,128)(2,1)S(1)}, u32[]{:S(2)}, u32[]{:S(2)}) collective-permute-start(bf16[128,2048]{1,0:T(8,128)(2,1)} %shard_map.73.own_ref.refs_0_), channel_id=1, source_target_pairs={{1,2},{3,4},{5,6},{7,8},{9,10},{11,12},{13,14},{15,0},{0,15},{2,1}... | collective-permute-start | bytes 1572872 | tf_op jit(solution)/shard_map/ppermute | solution.py:260
  9.0 1.9 %collective-permute-start = (bf16[128,2048]{1,0:T(8,128)(2,1)}, bf16[128,2048]{1,0:T(8,128)(2,1)S(1)}, u32[]{:S(2)}, u32[]{:S(2)}) collective-permute-start(bf16[128,2048]{1,0:T(8,128)(2,1)} %shard_map.73.own_ref.refs_0_), channel_id=1, source_target_pairs={{0,1},{1,0},{2,3},{3,2},{4,5},{5,4},{6,7},{7,6},{8,9},{9,8},{10,11... | collective-permute-start | bytes 1572872 | tf_op jit(solution)/shard_map/ppermute | solution.py:260
  10.9 3.0 %collective-permute-done.2 = bf16[128,2048]{1,0:T(8,128)(2,1)S(1)} collective-permute-done((bf16[128,2048]{1,0:T(8,128)(2,1)}, bf16[128,2048]{1,0:T(8,128)(2,1)S(1)}, u32[]{:S(2)}, u32[]{:S(2)}) %collective-permute-start.2) | collective-permute-done | bytes 524320 | tf_op jit(solution)/shard_map/ppermute | solution.py:260
  13.9 2.6 %collective-permute-start.4 = (bf16[128,2048]{1,0:T(8,128)(2,1)S(1)}, bf16[128,2048]{1,0:T(8,128)(2,1)S(1)}, u32[]{:S(2)}, u32[]{:S(2)}) collective-permute-start(bf16[128,2048]{1,0:T(8,128)(2,1)S(1)} %collective-permute-done.2), channel_id=1, source_target_pairs={{0,2},{2,4},{4,6},{6,8},{8,10},{10,12},{12,14},{14,0},{1,15},{3,1}... | collective-permute-start | bytes 1572872 | tf_op jit(solution)/shard_map/ppermute | solution.py:260
  16.5 0.8 %copy.14 = s32[1,32,4]{2,1,0:T(8,128)S(1)} copy(s32[1,32,4]{1,2,0:T(4,128)} %param.12) | data formatting | bytes 1024 | tf_op args[5]
  17.4 0.8 %collective-permute-done.1.got_ref = bf16[128,2048]{1,0:T(8,128)(2,1)S(1)} collective-permute-done((bf16[128,2048]{1,0:T(8,128)(2,1)}, bf16[128,2048]{1,0:T(8,128)(2,1)S(1)}, u32[]{:S(2)}, u32[]{:S(2)}) %collective-permute-start.1) | collective-permute-done | bytes 524320 | tf_op jit(solution)/shard_map/ppermute | solution.py:260
  18.2 3.4 %collective-permute-start.5 = (bf16[128,2048]{1,0:T(8,128)(2,1)S(1)}, bf16[128,2048]{1,0:T(8,128)(2,1)S(1)}, u32[]{:S(2)}, u32[]{:S(2)}) collective-permute-start(bf16[128,2048]{1,0:T(8,128)(2,1)S(1)} %collective-permute-done.1.got_ref), channel_id=1, source_target_pairs={{0,2},{2,4},{4,6},{6,8},{8,10},{10,12},{12,14},{14,0},{1,15},{3,1}... | collective-permute-start | bytes 1572872 | tf_op jit(solution)/shard_map/ppermute | solution.py:260
  21.6 1.0 %copy-done = bf16[128,2048]{1,0:T(8,128)(2,1)S(1)} copy-done((bf16[128,2048]{1,0:T(8,128)(2,1)S(1)}, bf16[128,2048]{1,0:T(8,128)(2,1)}, u32[]{:S(2)}) %copy-start) | copy-done | bytes 524312
  22.7 1.2 %copy-done.2 = bf16[128,4096]{1,0:T(8,128)(2,1)S(1)} copy-done((bf16[128,4096]{1,0:T(8,128)(2,1)S(1)}, bf16[128,4096]{1,0:T(8,128)(2,1)}, u32[]{:S(2)}) %copy-start.2) | copy-done | bytes 1048600
  24.5 3.0 %shard_map.74 = (f32[128,4096]{1,0:T(8,128)S(1)}, f32[128,4096]{1,0:T(8,128)S(1)}, f32[128,4096]{1,0:T(8,128)S(1)}, s32[80]{0:T(128)S(1)}) custom-call(s32[1]{0:T(128)} %bitcast.me_ref, s32[128]{0:T(128)S(1)} %copy-done.4, s32[128]{0:T(128)S(1)} %reshape.7.lists_ref, bf16[128,4096]{1,0:T(8,128)(2,1)S(1)} %copy-done.2, bf16[128,2048]{1,0:T(8,128)(2,1)S(1)} %copy-done, ...), custom_call_target="tpu_custom_call" | custom-call | flops 536870912 | bytes 4194304 | tf_op jit(solution)/shard_map/pallas_call | solution.py:164
  27.6 1.9 %collective-permute-start.7 = (bf16[128,2048]{1,0:T(8,128)(2,1)S(1)}, bf16[128,2048]{1,0:T(8,128)(2,1)S(1)}, u32[]{:S(2)}, u32[]{:S(2)}) collective-permute-start(bf16[128,2048]{1,0:T(8,128)(2,1)S(1)} %shard_map.75), channel_id=1, source_target_pairs={{0,2},{2,4},{4,6},{6,8},{8,10},{10,12},{12,14},{14,0},{1,15},{3,1}... | collective-permute-start | bytes 1572872 | tf_op jit(solution)/shard_map/ppermute | solution.py:260
  29.6 7.5 %collective-permute-start.3 = (bf16[128,4096]{1,0:T(8,128)(2,1)S(1)}, bf16[128,4096]{1,0:T(8,128)(2,1)S(1)}, u32[]{:S(2)}, u32[]{:S(2)}) collective-permute-start(bf16[128,4096]{1,0:T(8,128)(2,1)S(1)} %constant_dynamic-update-slice_fusion.refs_2_), channel_id=1, source_target_pairs={{0,1},{1,0},{2,3},{3,2},{4,5},{5,4},{6,7},{7,6},{8,9},{9,8},{10,11... | collective-permute-start | bytes 3145736 | tf_op jit(solution)/shard_map/ppermute | solution.py:260
  37.1 2.5 %collective-permute-start.8 = (bf16[128,2048]{1,0:T(8,128)(2,1)S(1)}, bf16[128,2048]{1,0:T(8,128)(2,1)S(1)}, u32[]{:S(2)}, u32[]{:S(2)}) collective-permute-start(bf16[128,2048]{1,0:T(8,128)(2,1)S(1)} %collective-permute-done.5), channel_id=1, source_target_pairs={{0,2},{2,4},{4,6},{6,8},{8,10},{10,12},{12,14},{14,0},{1,15},{3,1}... | collective-permute-start | bytes 1572872 | tf_op jit(solution)/shard_map/ppermute | solution.py:260
  39.7 2.6 %collective-permute-start.6 = (bf16[128,4096]{1,0:T(8,128)(2,1)S(1)}, bf16[128,4096]{1,0:T(8,128)(2,1)S(1)}, u32[]{:S(2)}, u32[]{:S(2)}) collective-permute-start(bf16[128,4096]{1,0:T(8,128)(2,1)S(1)} %pad_maximum_fusion.refs_4_), channel_id=1, source_target_pairs={{0,1},{1,0},{2,3},{3,2},{4,5},{5,4},{6,7},{7,6},{8,9},{9,8},{10,11... | collective-permute-start | bytes 3145736 | tf_op jit(solution)/shard_map/ppermute | solution.py:260
  42.3 3.6 %collective-permute-start.10 = (bf16[128,1024]{1,0:T(8,128)(2,1)S(1)}, bf16[128,1024]{1,0:T(8,128)(2,1)S(1)}, u32[]{:S(2)}, u32[]{:S(2)}) collective-permute-start(bf16[128,1024]{1,0:T(8,128)(2,1)S(1)} %get-tuple-element.14), channel_id=1, source_target_pairs={{0,2},{2,4},{4,6},{6,8},{8,10},{10,12},{12,14},{14,0},{1,15},{3,1}... | collective-permute-start | bytes 786440 | tf_op jit(solution)/shard_map/ppermute | solution.py:260
  46.0 1.4 %collective-permute-done.8 = bf16[128,2048]{1,0:T(8,128)(2,1)S(1)} collective-permute-done((bf16[128,2048]{1,0:T(8,128)(2,1)S(1)}, bf16[128,2048]{1,0:T(8,128)(2,1)S(1)}, u32[]{:S(2)}, u32[]{:S(2)}) %collective-permute-start.8) | collective-permute-done | bytes 524320 | tf_op jit(solution)/shard_map/ppermute | solution.py:260
  48.2 5.7 %collective-permute-start.9 = (bf16[128,4096]{1,0:T(8,128)(2,1)S(1)}, bf16[128,4096]{1,0:T(8,128)(2,1)S(1)}, u32[]{:S(2)}, u32[]{:S(2)}) collective-permute-start(bf16[128,4096]{1,0:T(8,128)(2,1)S(1)} %constant_dynamic-update-slice_fusion.2.refs_6_), channel_id=1, source_target_pairs={{0,1},{1,0},{2,3},{3,2},{4,5},{5,4},{6,7},{7,6},{8,9},{9,8},{10,11... | collective-permute-start | bytes 3145736 | tf_op jit(solution)/shard_map/ppermute | solution.py:260
  54.0 1.3 %collective-permute-start.13 = (bf16[128,2048]{1,0:T(8,128)(2,1)S(1)}, bf16[128,2048]{1,0:T(8,128)(2,1)S(1)}, u32[]{:S(2)}, u32[]{:S(2)}) collective-permute-start(bf16[128,2048]{1,0:T(8,128)(2,1)S(1)} %collective-permute-done.12.refs_10_), channel_id=1, source_target_pairs={{8,9},{10,11},{12,13},{14,15},{24,25},{26,27},{28,29},{30,31},{40,... | collective-permute-start | bytes 1572872 | tf_op jit(solution)/shard_map/ppermute | solution.py:260
  55.3 0.9 %collective-permute-done.9.after.refs_7_ = bf16[128,4096]{1,0:T(8,128)(2,1)S(1)} collective-permute-done((bf16[128,4096]{1,0:T(8,128)(2,1)S(1)}, bf16[128,4096]{1,0:T(8,128)(2,1)S(1)}, u32[]{:S(2)}, u32[]{:S(2)}) %collective-permute-start.9) | collective-permute-done | bytes 1048608 | tf_op jit(solution)/shard_map/ppermute | solution.py:260
  56.2 9.0 %collective-permute-start.11 = (bf16[128,1024]{1,0:T(8,128)(2,1)S(1)}, bf16[128,1024]{1,0:T(8,128)(2,1)S(1)}, u32[]{:S(2)}, u32[]{:S(2)}) collective-permute-start(bf16[128,1024]{1,0:T(8,128)(2,1)S(1)} %shard_map.78), channel_id=1, source_target_pairs={{0,1},{1,0},{2,3},{3,2},{4,5},{5,4},{6,7},{7,6},{8,9},{9,8},{10,11... | collective-permute-start | bytes 786440 | tf_op jit(solution)/shard_map/ppermute | solution.py:260
  65.2 1.1 %collective-permute-done.11.refs_9_ = bf16[128,1024]{1,0:T(8,128)(2,1)S(1)} collective-permute-done((bf16[128,1024]{1,0:T(8,128)(2,1)S(1)}, bf16[128,1024]{1,0:T(8,128)(2,1)S(1)}, u32[]{:S(2)}, u32[]{:S(2)}) %collective-permute-start.11) | collective-permute-done | bytes 262176 | tf_op jit(solution)/shard_map/ppermute | solution.py:260
  66.3 5.2 %shard_map.80 = bf16[128,4096]{1,0:T(8,128)(2,1)} custom-call(s32[80]{0:T(128)S(1)} %get-tuple-element.9.after.place_ref, bf16[128,4096]{1,0:T(8,128)(2,1)S(1)} %copy-done.3, f32[128,4096]{1,0:T(8,128)S(1)} %get-tuple-element.10.total_ref, f32[128,4096]{1,0:T(8,128)S(1)} %get-tuple-element.11.sum_ref, f32[128,4096]{1,0:T(8,128)S(1)} %get-tuple-element.12.top_ref, ...), custom_call_target="tpu_custom_call" | custom-call | flops 536870912 | bytes 6291456 | tf_op jit(solution)/shard_map/pallas_call | solution.py:240
  (33 shorter events, 1.8 us)
Async XLA Ops:
  1.9 12.0 %collective-permute-start.2 = (bf16[128,2048]{1,0:T(8,128)(2,1)}, bf16[128,2048]{1,0:T(8,128)(2,1)S(1)}, u32[]{:S(2)}, u32[]{:S(2)}) collective-permute-start(bf16[128,2048]{1,0:T(8,128)(2,1)} %shard_map.73.own_ref.refs_0_), channel_id=1, source_target_pairs={{0,2},{2,4},{4,6},{6,8},{8,10},{10,12},{12,14},{14,0},{1,15},{3,1}... | collective-permute-start | bytes 1572872 | tf_op jit(solution)/shard_map/ppermute | solution.py:260
  3.9 14.4 %collective-permute-start.1 = (bf16[128,2048]{1,0:T(8,128)(2,1)}, bf16[128,2048]{1,0:T(8,128)(2,1)S(1)}, u32[]{:S(2)}, u32[]{:S(2)}) collective-permute-start(bf16[128,2048]{1,0:T(8,128)(2,1)} %shard_map.73.own_ref.refs_0_), channel_id=1, source_target_pairs={{1,2},{3,4},{5,6},{7,8},{9,10},{11,12},{13,14},{15,0},{0,15},{2,1}... | collective-permute-start | bytes 1572872 | tf_op jit(solution)/shard_map/ppermute | solution.py:260
  9.0 12.6 %collective-permute-start = (bf16[128,2048]{1,0:T(8,128)(2,1)}, bf16[128,2048]{1,0:T(8,128)(2,1)S(1)}, u32[]{:S(2)}, u32[]{:S(2)}) collective-permute-start(bf16[128,2048]{1,0:T(8,128)(2,1)} %shard_map.73.own_ref.refs_0_), channel_id=1, source_target_pairs={{0,1},{1,0},{2,3},{3,2},{4,5},{5,4},{6,7},{7,6},{8,9},{9,8},{10,11... | collective-permute-start | bytes 1572872 | tf_op jit(solution)/shard_map/ppermute | solution.py:260
  13.9 13.7 %collective-permute-start.4 = (bf16[128,2048]{1,0:T(8,128)(2,1)S(1)}, bf16[128,2048]{1,0:T(8,128)(2,1)S(1)}, u32[]{:S(2)}, u32[]{:S(2)}) collective-permute-start(bf16[128,2048]{1,0:T(8,128)(2,1)S(1)} %collective-permute-done.2), channel_id=1, source_target_pairs={{0,2},{2,4},{4,6},{6,8},{8,10},{10,12},{12,14},{14,0},{1,15},{3,1}... | collective-permute-start | bytes 1572872 | tf_op jit(solution)/shard_map/ppermute | solution.py:260
  18.2 18.9 %collective-permute-start.5 = (bf16[128,2048]{1,0:T(8,128)(2,1)S(1)}, bf16[128,2048]{1,0:T(8,128)(2,1)S(1)}, u32[]{:S(2)}, u32[]{:S(2)}) collective-permute-start(bf16[128,2048]{1,0:T(8,128)(2,1)S(1)} %collective-permute-done.1.got_ref), channel_id=1, source_target_pairs={{0,2},{2,4},{4,6},{6,8},{8,10},{10,12},{12,14},{14,0},{1,15},{3,1}... | collective-permute-start | bytes 1572872 | tf_op jit(solution)/shard_map/ppermute | solution.py:260
  21.6 1.0 %copy-start = (bf16[128,2048]{1,0:T(8,128)(2,1)S(1)}, bf16[128,2048]{1,0:T(8,128)(2,1)}, u32[]{:S(2)}) copy-start(bf16[128,2048]{1,0:T(8,128)(2,1)} %shard_map.73.own_ref.refs_0_) | copy-start | bytes 1572868
  22.7 1.2 %copy-start.2 = (bf16[128,4096]{1,0:T(8,128)(2,1)S(1)}, bf16[128,4096]{1,0:T(8,128)(2,1)}, u32[]{:S(2)}) copy-start(bf16[128,4096]{1,0:T(8,128)(2,1)} %q_ref.3) | copy-start | bytes 3145732
  23.9 0.7 copy-start.4
  27.6 14.7 %collective-permute-start.7 = (bf16[128,2048]{1,0:T(8,128)(2,1)S(1)}, bf16[128,2048]{1,0:T(8,128)(2,1)S(1)}, u32[]{:S(2)}, u32[]{:S(2)}) collective-permute-start(bf16[128,2048]{1,0:T(8,128)(2,1)S(1)} %shard_map.75), channel_id=1, source_target_pairs={{0,2},{2,4},{4,6},{6,8},{8,10},{10,12},{12,14},{14,0},{1,15},{3,1}... | collective-permute-start | bytes 1572872 | tf_op jit(solution)/shard_map/ppermute | solution.py:260
  29.6 35.7 %collective-permute-start.3 = (bf16[128,4096]{1,0:T(8,128)(2,1)S(1)}, bf16[128,4096]{1,0:T(8,128)(2,1)S(1)}, u32[]{:S(2)}, u32[]{:S(2)}) collective-permute-start(bf16[128,4096]{1,0:T(8,128)(2,1)S(1)} %constant_dynamic-update-slice_fusion.refs_2_), channel_id=1, source_target_pairs={{0,1},{1,0},{2,3},{3,2},{4,5},{5,4},{6,7},{7,6},{8,9},{9,8},{10,11... | collective-permute-start | bytes 3145736 | tf_op jit(solution)/shard_map/ppermute | solution.py:260
  37.1 10.2 %collective-permute-start.8 = (bf16[128,2048]{1,0:T(8,128)(2,1)S(1)}, bf16[128,2048]{1,0:T(8,128)(2,1)S(1)}, u32[]{:S(2)}, u32[]{:S(2)}) collective-permute-start(bf16[128,2048]{1,0:T(8,128)(2,1)S(1)} %collective-permute-done.5), channel_id=1, source_target_pairs={{0,2},{2,4},{4,6},{6,8},{8,10},{10,12},{12,14},{14,0},{1,15},{3,1}... | collective-permute-start | bytes 1572872 | tf_op jit(solution)/shard_map/ppermute | solution.py:260
  39.7 15.6 %collective-permute-start.6 = (bf16[128,4096]{1,0:T(8,128)(2,1)S(1)}, bf16[128,4096]{1,0:T(8,128)(2,1)S(1)}, u32[]{:S(2)}, u32[]{:S(2)}) collective-permute-start(bf16[128,4096]{1,0:T(8,128)(2,1)S(1)} %pad_maximum_fusion.refs_4_), channel_id=1, source_target_pairs={{0,1},{1,0},{2,3},{3,2},{4,5},{5,4},{6,7},{7,6},{8,9},{9,8},{10,11... | collective-permute-start | bytes 3145736 | tf_op jit(solution)/shard_map/ppermute | solution.py:260
  42.3 11.6 %collective-permute-start.10 = (bf16[128,1024]{1,0:T(8,128)(2,1)S(1)}, bf16[128,1024]{1,0:T(8,128)(2,1)S(1)}, u32[]{:S(2)}, u32[]{:S(2)}) collective-permute-start(bf16[128,1024]{1,0:T(8,128)(2,1)S(1)} %get-tuple-element.14), channel_id=1, source_target_pairs={{0,2},{2,4},{4,6},{6,8},{8,10},{10,12},{12,14},{14,0},{1,15},{3,1}... | collective-permute-start | bytes 786440 | tf_op jit(solution)/shard_map/ppermute | solution.py:260
  47.4 6.6 %collective-permute-start.12 = (bf16[128,2048]{1,0:T(8,128)(2,1)S(1)}, bf16[128,2048]{1,0:T(8,128)(2,1)S(1)}, u32[]{:S(2)}, u32[]{:S(2)}) collective-permute-start(bf16[128,2048]{1,0:T(8,128)(2,1)S(1)} %pad_maximum_fusion.1), channel_id=1, source_target_pairs={{6,8},{8,10},{10,12},{12,14},{22,24},{24,26},{26,28},{28,30},{38,4... | collective-permute-start | bytes 1572872 | tf_op jit(solution)/shard_map/ppermute | solution.py:260
  48.2 8.0 %collective-permute-start.9 = (bf16[128,4096]{1,0:T(8,128)(2,1)S(1)}, bf16[128,4096]{1,0:T(8,128)(2,1)S(1)}, u32[]{:S(2)}, u32[]{:S(2)}) collective-permute-start(bf16[128,4096]{1,0:T(8,128)(2,1)S(1)} %constant_dynamic-update-slice_fusion.2.refs_6_), channel_id=1, source_target_pairs={{0,1},{1,0},{2,3},{3,2},{4,5},{5,4},{6,7},{7,6},{8,9},{9,8},{10,11... | collective-permute-start | bytes 3145736 | tf_op jit(solution)/shard_map/ppermute | solution.py:260
  54.0 11.2 %collective-permute-start.13 = (bf16[128,2048]{1,0:T(8,128)(2,1)S(1)}, bf16[128,2048]{1,0:T(8,128)(2,1)S(1)}, u32[]{:S(2)}, u32[]{:S(2)}) collective-permute-start(bf16[128,2048]{1,0:T(8,128)(2,1)S(1)} %collective-permute-done.12.refs_10_), channel_id=1, source_target_pairs={{8,9},{10,11},{12,13},{14,15},{24,25},{26,27},{28,29},{30,31},{40,... | collective-permute-start | bytes 1572872 | tf_op jit(solution)/shard_map/ppermute | solution.py:260
  56.2 10.2 %copy-start.1 = (bf16[128,2048]{1,0:T(8,128)(2,1)S(1)}, bf16[128,2048]{1,0:T(8,128)(2,1)}, u32[]{:S(2)}) copy-start(bf16[128,2048]{1,0:T(8,128)(2,1)} %shard_map.73.own_ref.refs_0_) | copy-start | bytes 1572868
  56.2 10.2 %copy-start.3 = (bf16[128,4096]{1,0:T(8,128)(2,1)S(1)}, bf16[128,4096]{1,0:T(8,128)(2,1)}, u32[]{:S(2)}) copy-start(bf16[128,4096]{1,0:T(8,128)(2,1)} %q_ref.3) | copy-start | bytes 3145732
  56.2 10.2 %collective-permute-start.11 = (bf16[128,1024]{1,0:T(8,128)(2,1)S(1)}, bf16[128,1024]{1,0:T(8,128)(2,1)S(1)}, u32[]{:S(2)}, u32[]{:S(2)}) collective-permute-start(bf16[128,1024]{1,0:T(8,128)(2,1)S(1)} %shard_map.78), channel_id=1, source_target_pairs={{0,1},{1,0},{2,3},{3,2},{4,5},{5,4},{6,7},{7,6},{8,9},{9,8},{10,11... | collective-permute-start | bytes 786440 | tf_op jit(solution)/shard_map/ppermute | solution.py:260
